TPU v7x, 32 devices: a whole 2x2x4 slice. The times are simulated.
32 devices in a mesh: group: 2 (over y), chan: 4 (over z), stat: 2 (over x), pol: 2 (over core).
Axes of the slice: x: 2, y: 2, z: 4, core: 2. Of those that a mesh axis runs over, the one named last changes fastest.
Arguments:
- voltages: bfloat16 [4, 16, 2, 19, 2, 4096], P(('group', 'stat'), 'chan', 'pol'), parts along dimension 0, may hold values from -6 to 6
- filter_taps: float32 [12, 4096], replicated, may hold values from -1.5 to 1.5
- beam_table: float32 [2, 16], replicated, may hold values from -4 to 4
- beam_index: int32 [500, 32], replicated, may hold values from 0 to 15
- block_owner: int32 [32], replicated, may hold values from 0 to 31, each once
Outputs:
- visibilities: float32 [64, 2, 64, 64], P(('group', 'chan'), None, ('stat', 'pol')), parts along dimension 0
- beams: float32 [1000, 2, 2, 8, 4096], P(('group', 'stat'), 'pol', None, None, 'chan'), parts along dimension 0
There are 2 independent parts, one for each index of `group`. A program takes and returns all parts, laid end to end along the dimension named above; an argument that names none is the same for every part. Nothing has to cross between parts.
Inputs may be any that keep to these rules, and one draw needn't show every extreme that they name: `block_owner`: each of the 32 channel groups appears at exactly one position.
All inputs are finite; a program needn't handle non-finite values.
Results may differ from a plain program's by a relative error of at most 0.0095.
Values may be sent and summed in bfloat16 or wider, within the bound.
A program may use at most 64 MiB of HBM per device.

v0:
```python
import math

import jax
import jax.numpy as jnp
from jax import lax
from jax.sharding import PartitionSpec as P

ROOT = 64
AVG = 128


def fourier_segment(length):
    counter = jnp.arange(length, dtype=jnp.int32)
    phase = (counter[:, None] * counter[None, :] % length).astype(jnp.float32) * (
        2.0 * math.pi / length
    )
    cosine = jnp.cos(phase)
    sine = jnp.sin(phase)
    upper_half = jnp.stack([cosine, -sine], axis=1)
    lower_half = jnp.stack([sine, cosine], axis=1)
    return jnp.stack([upper_half, lower_half], axis=0)


def channelise(voltages, filter_taps):
    samples = voltages[0, :, 0].astype(jnp.float32)
    taps_count = filter_taps.shape[0]
    frames = samples.shape[1] - taps_count + 1
    filtered = filter_taps[0] * samples[:, 0:frames]
    for tap_index in range(1, taps_count):
        filtered = filtered + filter_taps[tap_index] * samples[:, tap_index : tap_index + frames]
    stations = samples.shape[0]
    shaped = filtered.reshape(stations, frames, 2, ROOT, ROOT)
    matrix = fourier_segment(ROOT)
    segment_one = jnp.einsum("sfcxy,cxdk->sfdky", shaped, matrix, precision=lax.Precision.HIGHEST)
    counter = jnp.arange(ROOT, dtype=jnp.int32)
    twiddle = (counter[:, None] * counter[None, :]).astype(jnp.float32) * (
        2.0 * math.pi / (ROOT * ROOT)
    )
    twiddle_cos = jnp.cos(twiddle)
    twiddle_sin = jnp.sin(twiddle)
    turned_real = segment_one[:, :, 0] * twiddle_cos + segment_one[:, :, 1] * twiddle_sin
    turned_imag = segment_one[:, :, 1] * twiddle_cos - segment_one[:, :, 0] * twiddle_sin
    turned = jnp.stack([turned_real, turned_imag], axis=2)
    segment_two = jnp.einsum("sfcky,cydz->sdfzk", turned, matrix, precision=lax.Precision.HIGHEST)
    return (segment_two.reshape(stations, 2, frames, ROOT * ROOT) * (1.0 / ROOT)).astype(
        jnp.bfloat16
    )


def beam_weights(indices, beam_table, factor):
    levels = jnp.arange(beam_table.shape[1], dtype=jnp.int32)
    selected = indices[..., None] == levels
    w_real = jnp.sum(jnp.where(selected, beam_table[0], 0.0), axis=-1) * factor
    w_imag = jnp.sum(jnp.where(selected, beam_table[1], 0.0), axis=-1) * factor
    upper_half = jnp.stack([w_real, -w_imag], axis=1)
    lower_half = jnp.stack([w_imag, w_real], axis=1)
    return jnp.stack([upper_half, lower_half], axis=1).astype(jnp.bfloat16)


def on_device(voltages, filter_taps, beam_table, beam_index, block_owner):
    spectra = channelise(voltages, filter_taps)
    stations = spectra.shape[0]
    frames = spectra.shape[2]
    nfft_total = spectra.shape[3]
    owners = lax.axis_size("chan")
    chan_width = nfft_total // owners
    group_count = block_owner.shape[0]
    grouped = spectra.reshape(stations, 2, frames, group_count, nfft_total // group_count)
    regrouped = jnp.take(grouped, block_owner, axis=3)
    ordered = regrouped.reshape(stations, 2, frames, owners, chan_width)
    exchanged = lax.all_to_all(ordered, "chan", split_axis=3, concat_axis=0, tiled=True)
    local_spectra = exchanged.reshape(-1, 2, frames, chan_width)
    section_rows = local_spectra.shape[0]
    sections = lax.axis_size("stat")
    input_count = section_rows * 2 * sections
    groups = chan_width // AVG
    mean_factor = 1.0 / (frames * AVG)
    own_rows = local_spectra.reshape(section_rows, 2, frames, groups, AVG)
    section = lax.axis_index("stat")
    polarity = lax.axis_index("pol")
    station_count = beam_index.shape[1]
    beam_count = beam_index.shape[0]
    owned_beams = beam_count // sections
    norm_factor = 1.0 / math.sqrt(station_count)
    own_index = lax.dynamic_slice_in_dim(beam_index, section * owned_beams, owned_beams, 0)
    own_weights = beam_weights(own_index, beam_table, norm_factor)
    spread = own_weights.reshape(owned_beams, 2, 2, sections, 1, section_rows)
    chosen = (jnp.arange(2, dtype=jnp.int32) == polarity).reshape(1, 1, 1, 1, 2, 1)
    spread = jnp.where(chosen, spread, jnp.zeros((), jnp.bfloat16))
    wide_weights = spread.reshape(owned_beams, 2, 2, input_count)
    shard_rows = lax.all_gather(local_spectra, ("stat", "pol"), axis=0, tiled=True)
    piece_rows = shard_rows.shape[0]
    beam_term = jnp.einsum(
        "bocj,jcq->boq",
        wide_weights,
        shard_rows.reshape(piece_rows, 2, -1),
        preferred_element_type=jnp.float32,
    )
    piece_rows = shard_rows.shape[0]
    rotated = jnp.concatenate([-shard_rows[:, 1:2], shard_rows[:, 0:1]], axis=1)
    their_rows = shard_rows.reshape(piece_rows, 2, frames, groups, AVG)
    their_turned = rotated.reshape(piece_rows, 2, frames, groups, AVG)
    real_part = jnp.einsum(
        "icfam,jcfam->aij", own_rows, their_rows, preferred_element_type=jnp.float32
    )
    imag_part = jnp.einsum(
        "icfam,jcfam->aij", own_rows, their_turned, preferred_element_type=jnp.float32
    )
    vis_block = jnp.stack([real_part, imag_part], axis=1) * mean_factor
    return (vis_block, beam_term.reshape(owned_beams, 1, 2, frames, chan_width))


def solution(mesh):
    return jax.shard_map(
        on_device,
        mesh=mesh,
        in_specs=(P(("group", "stat"), "chan", "pol", None, None, None), P(), P(), P(), P()),
        out_specs=(
            P(("group", "chan"), None, ("stat", "pol"), None),
            P(("group", "stat"), "pol", None, None, "chan"),
        ),
        check_vma=False,
    )
```

profile of v0, /device:TPU:0, one launch (start us, length us, event | category | flops | bytes accessed | tf_op | source)
XLA Modules:
  0.0 116.7 jit_solution(14907172509124150411)
XLA Ops:
  7.2 0.0 copy-start
  7.2 0.0 all-gather.2.cloned.1.call-start
  7.2 0.7 compare_and_fusion
  7.9 0.7 compare_select_fusion
  8.5 0.1 fusion.43
  8.7 0.1 fusion.41
  8.8 0.1 fusion.36
  9.0 0.1 broadcast_in_dim.60
  9.1 0.1 broadcast_bitcast_fusion
  9.2 2.1 %fusion.46 = (f32[1,4096]{1,0:T(1,128)S(1)}, f32[1,4096]{1,0:T(1,128)S(1)}, f32[1,4096]{1,0:T(1,128)S(1)}, f32[1,4096]{1,0:T(1,128)S(1)}, f32[1,4096]{1,0:T(1,12...) fusion(f32[12,4096]{1,0:T(8,128)} %param.6), kind=kLoop, calls=%fused_computation.89 | loop fusion | bytes 393216 | tf_op jit(solution)/shard_map/slice | solution.py:28
  11.3 2.4 %bitcast_convert_fusion = f32[4,19,2,4096]{3,2,1,0:T(2,128)S(1)} fusion(bf16[1,4,1,19,2,4096]{5,4,3,2,1,0:T(2,128)(2,1)} %param.5), kind=kLoop, calls=%fused_computation.17 | loop fusion | flops 622592 | bytes 3735552 | tf_op jit(solution)/shard_map/convert_element_type | solution.py:25
  13.6 6.6 %fusion.20 = f32[4,8,2,4096]{3,2,1,0:T(2,128)S(1)} fusion(f32[4,19,2,4096]{3,2,1,0:T(2,128)S(1)} %bitcast_convert_fusion, f32[4096]{0:T(1024)S(1)} %bitcast.152, f32[4096]{0:T(1024)S(1)} %bitcast.153, f32[4096]{0:T(1024)S(1)} %bitcast.143, f32[4096]{0:T(1024)S(1)} %bitcast.144, f32[4096]{0:T(1024)S(1)} %bitcast.145, f32[4096]{0:T(1024)S(1)} %bitcast.146, ...), kind=kLoop, calls=%fused_computation.22 | loop fusion | flops 6029312 | bytes 13828096 | tf_op jit(solution)/shard_map/add | solution.py:30
  20.3 1.2 %reshape.261 = f32[4,8,2,64,64,1]{4,3,2,1,0,5:T(8,128)S(1)} reshape(f32[4,8,2,4096]{3,2,1,0:T(2,128)S(1)} %fusion.20) | data formatting | bytes 2097152 | tf_op jit(solution)/shard_map/reshape | solution.py:32
  21.5 2.0 %convolution_bitcast_fusion.1 = f32[4,8,2,64,64]{4,3,1,0,2:T(8,128)S(1)} fusion(f32[4,8,2,64,64,1]{4,3,2,1,0,5:T(8,128)S(1)} %reshape.261, f32[1,64,2,64]{1,3,0,2:T(8,128)S(1)} %get-tuple-element.33, f32[1,64,2,64]{1,3,0,2:T(8,128)S(1)} %get-tuple-element.32), kind=kOutput, calls=%fused_computation.15 | convolution fusion | flops 402669568 | bytes 2162688 | tf_op jit(solution)/shard_map/sfcxy,cxdk->sfdky/dot_general | solution.py:34
  23.4 0.4 multiply_add_fusion
  23.8 3.1 %fusion.11 = bf16[4,2,8,64,64]{4,3,2,0,1:T(8,128)(2,1)S(1)} fusion(f32[1,64,2,64]{1,3,0,2:T(8,128)S(1)} %get-tuple-element.33, f32[1,64,2,64]{1,3,0,2:T(8,128)S(1)} %get-tuple-element.32, f32[4,8,1,64,64]{4,3,1,0,2:T(8,128)S(1)} %get-tuple-element.15, f32[4,8,1,64,64]{4,3,1,0,2:T(8,128)S(1)} %get-tuple-element.14), kind=kOutput, calls=%fused_computation.16 | convolution fusion | flops 403456000 | bytes 1638400 | tf_op jit(solution)/shard_map/sfcky,cydz->sdfzk/dot_general | solution.py:44
  27.0 0.5 convert_element_type.67
  27.5 0.2 copy.55
  27.7 0.8 gather_fusion
  28.5 0.3 copy.56
  28.8 0.1 gather.7
  29.0 0.0 copy-start.3
  29.0 0.2 broadcast_select_fusion
  29.2 0.2 copy.57
  29.4 20.7 %all_to_all.15 = bf16[4,2,8,4,1024]{4,2,1,0,3:T(8,128)(2,1)} all-to-all(bf16[4,2,8,4,1024]{4,2,1,0,3:T(8,128)(2,1)S(1)} %copy.57), channel_id=1, replica_groups=mesh['group'=2,'chan'=4,'stat'=2,'pol'=2] {'chan'}, dimensions={3} | all-to-all | bytes 1048576 | tf_op jit(solution)/shard_map/all_to_all | solution.py:71
  50.1 0.0 all-gather.2.cloned.1.call-update
  50.1 0.0 copy-done
  50.2 0.1 constant_dynamic-slice_fusion
  50.2 0.0 copy-done.3
  50.2 0.3 select_reduce_fusion
  50.6 0.1 broadcast_select_fusion.1
  50.7 1.1 copy.77
  51.9 20.1 %all-gather.2.cloned.1.call-done = bf16[64,2,8,1024]{3,2,1,0:T(8,128)(2,1)} async-done(((bf16[16,2,8,1024]{3,2,1,0:T(8,128)(2,1)}), bf16[64,2,8,1024]{3,2,1,0:T(8,128)(2,1)}) %all-gather.2.cloned.1.call-update) | async-done | bytes 2097168 | tf_op jit(solution)/shard_map/all_gather | solution.py:91
  72.0 0.0 copy-start.1
  72.0 3.7 %copy.78 = bf16[128,8,8,128]{3,2,1,0:T(8,128)(2,1)} copy(bf16[128,8,8,128]{3,1,2,0:T(8,128)(2,1)} %bitcast.129) | data formatting | bytes 4194304
  75.7 0.0 copy-done.1
  75.7 2.7 %reshape.245 = bf16[64,2,8192]{2,1,0:T(2,128)(2,1)} reshape(bf16[64,2,8,1024]{3,2,1,0:T(8,128)(2,1)S(1)} %copy-done.1) | data formatting | bytes 4194304 | tf_op jit(solution)/shard_map/reshape | solution.py:96
  78.4 2.7 %copy.64 = bf16[64,2,8192]{2,0,1:T(8,128)(2,1)S(1)} copy(bf16[64,2,8192]{2,1,0:T(2,128)(2,1)} %reshape.245) | data formatting | bytes 4194304 | tf_op jit(solution)/shard_map/reshape | solution.py:96
  81.2 0.1 slice_negate_fusion
  81.3 0.2 pad_maximum_fusion.1
  81.5 0.0 copy-start.2
  81.5 0.6 copy.79
  82.2 0.9 copy-done.2
  83.1 1.5 %fusion.14 = f32[8,1,16,64]{3,2,0,1:T(8,128)S(1)} fusion(bf16[64,2,8,8,128]{4,3,2,1,0:T(8,128)(2,1)S(1)} %bitcast.134, bf16[16,2,8,8,128]{4,3,2,1,0:T(8,128)(2,1)S(1)} %bitcast.138), kind=kOutput, calls=%fused_computation.18 | convolution fusion | flops 33554432 | bytes 2654208 | tf_op jit(solution)/shard_map/icfam,jcfam->aij/dot_general | solution.py:103
  84.6 1.5 %fusion.17 = f32[8,1,16,64]{3,2,0,1:T(8,128)S(1)} fusion(bf16[64,2,8,8,128]{4,3,2,1,0:T(8,128)(2,1)S(1)} %bitcast.135, bf16[16,2,8,8,128]{4,3,2,1,0:T(8,128)(2,1)S(1)} %bitcast.139), kind=kOutput, calls=%fused_computation.19 | convolution fusion | flops 33554432 | bytes 2654208 | tf_op jit(solution)/shard_map/icfam,jcfam->aij/dot_general | solution.py:106
  86.1 0.7 copy.66
  86.7 2.4 %convolution_bitcast_fusion = f32[250,1,2,8,1024]{4,0,3,2,1:T(8,128)S(1)} fusion(bf16[250,2,2,64,1]{0,3,2,4,1:T(8,128)(2,1)S(1)} %bitcast.137, bf16[2,8,8,8,1024]{4,3,2,1,0:T(8,128)(2,1)S(1)} %bitcast.130), kind=kOutput, calls=%fused_computation.1 | convolution fusion | flops 1048576000 | bytes 18609152 | tf_op jit(solution)/shard_map/bocj,jcq->boq/dot_general | solution.py:93
  89.1 20.8 %copy.67 = f32[250,1,2,8,1024]{4,3,2,1,0:T(8,128)} copy(f32[250,1,2,8,1024]{4,0,3,2,1:T(8,128)S(1)} %convolution_bitcast_fusion) | data formatting | bytes 32768000
  (10 shorter events, 0.1 us)
Async XLA Ops:
  7.2 43.0 %copy-start = (s32[500,32]{0,1:T(8,128)S(1)}, s32[500,32]{0,1:T(8,128)}, u32[]{:S(2)}) copy-start(s32[500,32]{0,1:T(8,128)} %param.8) | copy-start | bytes 192004
  7.2 64.8 %all-gather.2.cloned.1.call-start = ((), (), s32[]{:S(2)}) async-start(), calls=%async_computation.1 | async-start | bytes 2621440 | tf_op jit(solution)/shard_map/all_gather | solution.py:91
  29.0 21.3 %copy-start.3 = (f32[2,16]{1,0:T(2,128)S(1)}, f32[2,16]{1,0:T(2,128)}, u32[]{:S(2)}) copy-start(f32[2,16]{1,0:T(2,128)} %param.7) | copy-start | bytes 388
  72.0 3.7 %copy-start.1 = (bf16[64,2,8,1024]{3,2,1,0:T(8,128)(2,1)S(1)}, bf16[64,2,8,1024]{3,2,1,0:T(8,128)(2,1)}, u32[]{:S(2)}) copy-start(bf16[64,2,8,1024]{3,2,1,0:T(8,128)(2,1)} %all-gather.2.cloned.1.call-done) | copy-start | bytes 6291460
  81.5 1.6 %copy-start.2 = (bf16[128,8,8,128]{3,2,1,0:T(8,128)(2,1)S(1)}, bf16[128,8,8,128]{3,2,1,0:T(8,128)(2,1)}, u32[]{:S(2)}) copy-start(bf16[128,8,8,128]{3,2,1,0:T(8,128)(2,1)} %copy.78) | copy-start | bytes 6291460
Sparse Core Ops, SparseCore 0:
  50.2 21.6 all-gather.1
where the time goes:
time: 117 us
  local copies, waits for them, and re-layouts  39 us (33%)
  blocking collectives  20.7 us (18%)
  waiting for transfers between devices  20.1 us (17%)
  between operations  14.3 us (12%)
  other arithmetic  12.2 us (10%)
  matrix products  10.4 us (9%)
    unnamed x15, local copies, waits for them, and re-layouts  27.9 us
    all_to_all x1, blocking collectives, on_device(): lax.all_to_all(ordered, 'chan', split_axis=3, concat_axis=0, tiled=True)  20.7 us
    all_gather x1, waiting for transfers between devices, on_device(): lax.all_gather(local_spectra, ('stat', 'pol'), axis=0, tiled=True)  20.1 us
    add x1, other arithmetic, channelise(): filtered + filter_taps[tap_index] * samples[:, tap_index:tap_index + frames]  6.62 us
    reshape x2, local copies, waits for them, and re-layouts, on_device(): shard_rows.reshape(piece_rows, 2, -1)  5.49 us
    dot_general x1, matrix products, channelise(): jnp.einsum('sfcky,cydz->sdfzk', turned, matrix, precision=lax.Precision.H...  3.13 us
    dot_general x1, matrix products, on_device(): jnp.einsum('bocj,jcq->boq', wide_weights, shard_rows.reshape(piece_rows,...  2.36 us
    convert_element_type x1, other arithmetic, channelise(): samples = voltages[0, :, 0].astype(jnp.float32)  2.36 us
  transfers between devices with their start and end apart: 1, of which 1 were waited for; matrix products, arithmetic and copies ran while one was open for 1% of the time, Pallas kernels for 0%

commit v1 on v0

v1 whole, which is shorter than its diff:
```python
import functools
import math

import jax
import jax.numpy as jnp
from jax import lax
from jax.experimental import pallas as pl
from jax.experimental.pallas import tpu as pltpu
from jax.sharding import PartitionSpec as P

ROOT = 64
AVG = 128
MESH = pl.DeviceIdType.MESH
VMEM_BYTES = 56 * 2**20


def fourier_segment(length):
    counter = jnp.arange(length, dtype=jnp.int32)
    phase = (counter[:, None] * counter[None, :] % length).astype(jnp.float32) * (
        2.0 * math.pi / length
    )
    cosine = jnp.cos(phase)
    sine = jnp.sin(phase)
    upper_half = jnp.stack([cosine, -sine], axis=1)
    lower_half = jnp.stack([sine, cosine], axis=1)
    return jnp.stack([upper_half, lower_half], axis=0)


def channelise(voltages, filter_taps):
    samples = voltages[0, :, 0].astype(jnp.float32)
    taps_count = filter_taps.shape[0]
    frames = samples.shape[1] - taps_count + 1
    filtered = filter_taps[0] * samples[:, 0:frames]
    for tap_index in range(1, taps_count):
        filtered = filtered + filter_taps[tap_index] * samples[:, tap_index : tap_index + frames]
    stations = samples.shape[0]
    shaped = filtered.reshape(stations, frames, 2, ROOT, ROOT)
    matrix = fourier_segment(ROOT)
    segment_one = jnp.einsum("sfcxy,cxdk->sfdky", shaped, matrix, precision=lax.Precision.HIGHEST)
    counter = jnp.arange(ROOT, dtype=jnp.int32)
    twiddle = (counter[:, None] * counter[None, :]).astype(jnp.float32) * (
        2.0 * math.pi / (ROOT * ROOT)
    )
    twiddle_cos = jnp.cos(twiddle)
    twiddle_sin = jnp.sin(twiddle)
    turned_real = segment_one[:, :, 0] * twiddle_cos + segment_one[:, :, 1] * twiddle_sin
    turned_imag = segment_one[:, :, 1] * twiddle_cos - segment_one[:, :, 0] * twiddle_sin
    turned = jnp.stack([turned_real, turned_imag], axis=2)
    segment_two = jnp.einsum("sfcky,cydz->sdfzk", turned, matrix, precision=lax.Precision.HIGHEST)
    return (segment_two.reshape(stations, 2, frames, ROOT * ROOT) * (1.0 / ROOT)).astype(
        jnp.bfloat16
    )


def exchange_kernel(owners, sections, y_ref, g_ref, zs, zr, xs, xr, cs, cr, own_sem):
    z = lax.axis_index("chan")
    st = lax.axis_index("stat")
    pol = lax.axis_index("pol")

    barrier = pltpu.get_barrier_semaphore()
    for o in range(1, owners):
        pl.semaphore_signal(barrier, inc=1, device_id={"chan": lax.rem(z + o, owners)}, device_id_type=MESH)
    for o in range(1, sections):
        pl.semaphore_signal(barrier, inc=1, device_id={"stat": lax.rem(st + o, sections)}, device_id_type=MESH)
    pl.semaphore_signal(barrier, inc=1, device_id={"pol": 1 - pol}, device_id_type=MESH)
    pl.semaphore_wait(barrier, owners + sections - 1)

    def to_owner(o):
        target = lax.rem(z + o, owners)
        return pltpu.make_async_remote_copy(
            src_ref=y_ref.at[target], dst_ref=g_ref.at[0, st, z],
            send_sem=zs.at[o], recv_sem=zr.at[z],
            device_id={"chan": target}, device_id_type=MESH)

    def from_owner(o):
        source = lax.rem(z - o + owners, owners)
        return pltpu.make_async_remote_copy(
            src_ref=y_ref.at[source], dst_ref=g_ref.at[0, st, source],
            send_sem=zs.at[o], recv_sem=zr.at[source],
            device_id={"chan": source}, device_id_type=MESH)

    def to_section(o, block):
        target = lax.rem(st + o, sections)
        return pltpu.make_async_remote_copy(
            src_ref=g_ref.at[0, st, block], dst_ref=g_ref.at[0, st, block],
            send_sem=xs.at[o, block], recv_sem=xr.at[st, block],
            device_id={"stat": target}, device_id_type=MESH)

    def from_section(o, block):
        source = lax.rem(st - o + sections, sections)
        return pltpu.make_async_remote_copy(
            src_ref=g_ref.at[0, source, block], dst_ref=g_ref.at[0, source, block],
            send_sem=xs.at[o, block], recv_sem=xr.at[source, block],
            device_id={"stat": source}, device_id_type=MESH)

    def to_core(o, block):
        source = lax.rem(st - o + sections, sections)
        return pltpu.make_async_remote_copy(
            src_ref=g_ref.at[0, source, block], dst_ref=g_ref.at[1, source, block],
            send_sem=cs.at[source, block], recv_sem=cr.at[source, block],
            device_id={"pol": 1 - pol}, device_id_type=MESH)

    own = pltpu.make_async_copy(y_ref.at[z], g_ref.at[0, st, z], own_sem)
    own.start()
    for o in range(1, owners):
        to_owner(o).start()
    for o in range(owners):
        block = lax.rem(z - o + owners, owners)
        if o == 0:
            own.wait()
        else:
            from_owner(o).wait_recv()
        for q in range(1, sections):
            to_section(q, block).start()
        to_core(0, block).start()
        if o:
            before = lax.rem(z - o + 1 + owners, owners)
            for q in range(1, sections):
                from_section(q, before).wait_recv()
                to_core(q, before).start()
    last = lax.rem(z + 1, owners)
    for q in range(1, sections):
        from_section(q, last).wait_recv()
        to_core(q, last).start()
    for o in range(owners):
        for q in range(sections):
            to_core(q, lax.rem(z - o + owners, owners)).wait()
    for o in range(1, owners):
        to_owner(o).wait_send()
    for o in range(owners):
        for q in range(1, sections):
            to_section(q, lax.rem(z - o + owners, owners)).wait_send()


def exchange(blocks, owners, sections):
    return pl.pallas_call(
        functools.partial(exchange_kernel, owners, sections),
        out_shape=jax.ShapeDtypeStruct((2, sections) + blocks.shape, blocks.dtype),
        in_specs=[pl.BlockSpec(memory_space=pl.ANY)],
        out_specs=pl.BlockSpec(memory_space=pl.ANY),
        scratch_shapes=[
            pltpu.SemaphoreType.DMA((owners,)),
            pltpu.SemaphoreType.DMA((owners,)),
            pltpu.SemaphoreType.DMA((sections, owners)),
            pltpu.SemaphoreType.DMA((sections, owners)),
            pltpu.SemaphoreType.DMA((sections, owners)),
            pltpu.SemaphoreType.DMA((sections, owners)),
            pltpu.SemaphoreType.DMA,
        ],
        compiler_params=pltpu.CompilerParams(collective_id=0, has_side_effects=True),
        name="exchange",
    )(blocks)


def iota(shape, dim):
    return lax.broadcasted_iota(jnp.int32, shape, dim)


def product_kernel(frames, stations, mean_factor, place_ref, w_ref, col_ref, g_ref, vis_ref, out_ref, x_ref):
    _, sections, owners, groups, rows, _ = g_ref.shape
    step = pl.program_id(0)
    depth = sections * owners * rows
    pair = 4 * stations

    @pl.when(step == 0)
    def _():
        for a in range(groups):
            x_ref[:, a * AVG : (a + 1) * AVG] = g_ref[0, :, :, a].reshape(depth, AVG)

    nb = w_ref.shape[1]
    wide = jnp.dot(w_ref[0], col_ref[...], preferred_element_type=jnp.float32)
    column = iota((frames, depth), 1)
    same = lax.rem(lax.div(column, 2 * stations), frames) == iota((frames, depth), 0)
    spread = jnp.where(same[None], wide[:, None, :], 0.0).reshape(nb * frames, depth)
    out_ref[...] = jnp.dot(spread.astype(jnp.bfloat16), x_ref[...], preferred_element_type=jnp.float32)

    @pl.when(step == pl.num_programs(0) - 1)
    def _():
        st = place_ref[0]
        pol = place_ref[1]
        m = owners * pair
        n = sections * owners * pair
        own_count = owners * stations
        row = iota((m, n), 0)
        col = iota((m, n), 1)
        par = 2 * stations
        same_par = lax.rem(lax.div(row, par), 2) == lax.rem(lax.div(col, par), 2)
        rc = lax.rem(row, 2)
        cc = lax.rem(col, 2)
        re_mask = jnp.where(same_par & (rc == cc), mean_factor, 0.0)
        im_mask = jnp.where(same_par & (rc != cc), jnp.where(rc == 1, mean_factor, -mean_factor), 0.0)

        def station(i):
            return lax.div(i, pair) * stations + lax.rem(lax.div(i, 2), stations)

        left = (station(iota((own_count, m), 1)) == iota((own_count, m), 0)).astype(jnp.float32)
        inputs = sections * 2 * own_count
        for p in range(2):
            q = jnp.where(pol == 0, p, 1 - p)
            i = iota((n, inputs), 0)
            sec = lax.div(i, m)
            where = sec * (2 * own_count) + q * own_count + station(lax.rem(i, m))
            right = (where == iota((n, inputs), 1)).astype(jnp.float32)
            halves = []
            for a in range(groups):
                raw = jnp.zeros((m, n), jnp.float32)
                for f in range(rows // pair):
                    mine = g_ref[0, st, :, a, f * pair : (f + 1) * pair].reshape(m, AVG)
                    theirs = g_ref[p, :, :, a, f * pair : (f + 1) * pair].reshape(n, AVG)
                    raw = raw + lax.dot_general(
                        mine, theirs, (((1,), (1,)), ((), ())), preferred_element_type=jnp.float32
                    )
                for mask in (re_mask, im_mask):
                    halves.append(
                        jnp.dot(left, raw * mask, precision=lax.Precision.HIGHEST, preferred_element_type=jnp.float32)
                    )
            total = jnp.dot(
                jnp.concatenate(halves, axis=0), right,
                precision=lax.Precision.HIGHEST, preferred_element_type=jnp.float32,
            ).reshape(groups, 2, own_count, inputs)
            if p == 0:
                vis_ref[...] = total
            else:
                vis_ref[...] += total


def products(gathered, weights, frames, stations, mean_factor):
    _, sections, owners, groups, rows, _ = gathered.shape
    depth = sections * owners * rows
    width = groups * AVG
    count = weights.shape[0]
    nb = 50
    while count % nb or nb * frames * depth > 400 * 1024:
        nb -= 1
    blocks = count // nb
    row = jnp.arange(weights.shape[1], dtype=jnp.int32)[:, None]
    col = jnp.arange(depth, dtype=jnp.int32)[None, :]
    names = (col % 2) * (sections * owners * stations) + (col // rows) * stations + (col // 2) % stations
    spread = (row == names).astype(jnp.bfloat16)
    place = jnp.stack([lax.axis_index("stat"), lax.axis_index("pol")]).astype(jnp.int32)
    own_count = owners * stations
    vis, beams = pl.pallas_call(
        functools.partial(product_kernel, frames, stations, mean_factor),
        grid=(blocks,),
        in_specs=[
            pl.BlockSpec(memory_space=pltpu.SMEM),
            pl.BlockSpec((1, nb, weights.shape[1]), lambda i: (i, 0, 0)),
            pl.BlockSpec(memory_space=pltpu.VMEM),
            pl.BlockSpec(memory_space=pltpu.VMEM),
        ],
        out_specs=[
            pl.BlockSpec(memory_space=pltpu.VMEM),
            pl.BlockSpec((nb * frames, width), lambda i: (i, 0)),
        ],
        out_shape=[
            jax.ShapeDtypeStruct((groups, 2, own_count, 2 * sections * own_count), jnp.float32),
            jax.ShapeDtypeStruct((count * frames, width), jnp.float32),
        ],
        scratch_shapes=[pltpu.VMEM((depth, width), jnp.bfloat16)],
        compiler_params=pltpu.CompilerParams(vmem_limit_bytes=VMEM_BYTES),
        name="products",
    )(place, weights.reshape(blocks, nb, weights.shape[1]), spread, gathered)
    return vis, beams


def beam_weights(indices, beam_table, factor):
    levels = jnp.arange(beam_table.shape[1], dtype=jnp.int32)
    selected = indices[..., None] == levels
    w_real = jnp.sum(jnp.where(selected, beam_table[0], 0.0), axis=-1) * factor
    w_imag = jnp.sum(jnp.where(selected, beam_table[1], 0.0), axis=-1) * factor
    upper_half = jnp.concatenate([w_real, -w_imag], axis=1)
    lower_half = jnp.concatenate([w_imag, w_real], axis=1)
    return jnp.stack([upper_half, lower_half], axis=1).astype(jnp.bfloat16)


def on_device(voltages, filter_taps, beam_table, beam_index, block_owner):
    owners = lax.axis_size("chan")
    sections = lax.axis_size("stat")
    spectra = channelise(voltages, filter_taps)
    stations, _, frames, nfft = spectra.shape
    group_count = block_owner.shape[0]
    grouped = spectra.reshape(stations, 2, frames, group_count, AVG)
    regrouped = jnp.take(grouped, block_owner, axis=3)
    groups = group_count // owners
    blocks = jnp.transpose(regrouped, (3, 2, 0, 1, 4)).reshape(
        owners, groups, frames * stations * 2, AVG
    )
    gathered = exchange(blocks, owners, sections)
    section = lax.axis_index("stat")
    beam_count, station_count = beam_index.shape
    owned = beam_count // sections
    own_index = lax.dynamic_slice_in_dim(beam_index, section * owned, owned, 0)
    weights = beam_weights(own_index, beam_table, 1.0 / math.sqrt(station_count))
    vis, beams = products(
        gathered, weights.reshape(owned * 2, 2 * station_count), frames, stations, 1.0 / (frames * AVG)
    )
    return vis, beams.reshape(owned, 1, 2, frames, groups * AVG)


def solution(mesh):
    return jax.shard_map(
        on_device,
        mesh=mesh,
        in_specs=(P(("group", "stat"), "chan", "pol", None, None, None), P(), P(), P(), P()),
        out_specs=(
            P(("group", "chan"), None, ("stat", "pol"), None),
            P(("group", "stat"), "pol", None, None, "chan"),
        ),
        check_vma=False,
    )
```

time: 117 us -> 69.2 us (0.59)
  Pallas kernels: 0 us -> 43.1 us
  local copies, waits for them, and re-layouts: 39 us -> 7.91 us
  blocking collectives: 20.7 us -> 0 us
  waiting for transfers between devices: 20.1 us -> 0 us
  between operations: 14.3 us -> 0.81 us
  matrix products: 10.4 us -> 5.09 us
    pallas_call x0 -> x2, Pallas kernels: none -> 43.1 us  [the longest x1 25.3 us: exchange(): pl.pallas_call(functools.partial(exchange_kernel, owners, sections), out_...]
    unnamed x15 -> x4, local copies, waits for them, and re-layouts: 27.9 us -> 0.01 us
    all_to_all x1 -> x0, blocking collectives: 20.7 us -> none  [on_device(): lax.all_to_all(ordered, 'chan', split_axis=3, concat_axis=0, tiled=True)]
    all_gather x1 -> x0, waiting for transfers between devices: 20.1 us -> none  [on_device(): lax.all_gather(local_spectra, ('stat', 'pol'), axis=0, tiled=True)]
    reshape x2 -> x0, local copies, waits for them, and re-layouts: 5.49 us -> none  [on_device(): shard_rows.reshape(piece_rows, 2, -1)]
    dot_general x3 -> x0, matrix products: 5.31 us -> none  [the longest x1 2.36 us: on_device(): jnp.einsum('bocj,jcq->boq', wide_weights, shard_rows.reshape(piece_rows,...]
    convert_element_type x1, other arithmetic: 2.36 us -> 1.06 us  [channelise(): samples = voltages[0, :, 0].astype(jnp.float32)]
  transfers between devices with their start and end apart: 1 -> 0, of which waited for: 1 -> 0; matrix products, arithmetic and copies ran while one was open for 1% -> 0% of each run, Pallas kernels for 0% -> 0%
where the time goes in v1:
time: 69.2 us; the launch traced here: 68.7 us
  Pallas kernels  43.1 us (62%)
  other arithmetic  11.8 us (17%)
  local copies, waits for them, and re-layouts  7.91 us (11%)
  matrix products  5.09 us (7%)
  between operations  0.81 us (1%)
    pallas_call x1, Pallas kernels, exchange(): pl.pallas_call(functools.partial(exchange_kernel, owners, sections), out_...  25.3 us
    pallas_call x1, Pallas kernels, products(): pl.pallas_call(functools.partial(product_kernel, frames, stations, mean_f...  17.8 us
    add x1, other arithmetic, channelise(): filtered + filter_taps[tap_index] * samples[:, tap_index:tap_index + frames]  6.8 us
    dot_general x1, matrix products, channelise(): jnp.einsum('sfcky,cydz->sdfzk', turned, matrix, precision=lax.Precision.H...  3.13 us
    slice x1, local copies, waits for them, and re-layouts, channelise(): filtered = filter_taps[0] * samples[:, 0:frames]  2.1 us
    dot_general x1, matrix products, channelise(): jnp.einsum('sfcxy,cxdk->sfdky', shaped, matrix, precision=lax.Precision.H...  1.96 us

profile of v1, /device:TPU:0, one launch (start us, length us, event | category | flops | bytes accessed | tf_op | source)
XLA Modules:
  0.0 68.7 jit_solution(14751081415975961895)
XLA Ops:
  0.6 0.0 copy-start
  0.6 0.0 copy-start.1
  0.7 0.7 pad_add_fusion.place_ref
  1.3 0.7 compare_and_fusion
  2.0 0.7 compare_select_fusion
  2.6 0.8 %slice_bitcast_fusion.1 = (f32[16]{0:T(128)S(1)}, f32[16]{0:T(128)S(1)}) fusion(f32[2,16]{1,0:T(2,128)} %param.7), kind=kLoop, calls=%fused_computation.93 | loop fusion | bytes 256 | tf_op jit(solution)/shard_map/squeeze | solution.py:269
  3.4 0.0 copy-done
  3.4 0.1 constant_dynamic-slice_fusion
  3.5 0.3 select_reduce_fusion
  3.9 0.1 fusion.31
  4.0 0.1 copy.19
  4.1 0.9 %convert_element_type.64.w_ref = bf16[10,50,64]{2,1,0:T(8,128)(2,1)} reshape(bf16[250,2,64]{2,1,0:T(2,128)(2,1)S(1)} %copy.19) | data formatting | bytes 128000 | tf_op jit(solution)/shard_map/convert_element_type | solution.py:273
  5.0 0.6 fusion.20.col_ref
  5.6 0.1 fusion.29
  5.8 0.1 fusion.24
  5.9 2.1 %fusion.47 = (f32[1,4096]{1,0:T(1,128)S(1)}, f32[1,4096]{1,0:T(1,128)S(1)}, f32[1,4096]{1,0:T(1,128)S(1)}, f32[1,4096]{1,0:T(1,128)S(1)}, f32[1,4096]{1,0:T(1,12...) fusion(f32[12,4096]{1,0:T(8,128)} %param.6), kind=kLoop, calls=%fused_computation.97 | loop fusion | bytes 393216 | tf_op jit(solution)/shard_map/slice | solution.py:33
  8.0 0.0 copy-done.1
  8.1 1.1 %bitcast_convert_fusion = f32[4,19,2,4096]{3,2,1,0:T(2,128)S(1)} fusion(bf16[1,4,1,19,2,4096]{5,4,3,2,1,0:T(2,128)(2,1)S(1)} %copy-done.1), kind=kLoop, calls=%fused_computation.9 | loop fusion | flops 622592 | bytes 3735552 | tf_op jit(solution)/shard_map/convert_element_type | solution.py:30
  9.1 6.8 %fusion.9 = f32[4,8,2,4096]{3,2,1,0:T(2,128)S(1)} fusion(f32[4,19,2,4096]{3,2,1,0:T(2,128)S(1)} %bitcast_convert_fusion, f32[4096]{0:T(1024)S(1)} %bitcast.80, f32[4096]{0:T(1024)S(1)} %bitcast.81, f32[4096]{0:T(1024)S(1)} %bitcast.71, f32[4096]{0:T(1024)S(1)} %bitcast.72, f32[4096]{0:T(1024)S(1)} %bitcast.73, f32[4096]{0:T(1024)S(1)} %bitcast.74, ...), kind=kLoop, calls=%fused_computation.11 | loop fusion | flops 6029312 | bytes 13828096 | tf_op jit(solution)/shard_map/add | solution.py:35
  15.9 1.2 %reshape.262 = f32[4,8,2,64,64,1]{4,3,2,1,0,5:T(8,128)S(1)} reshape(f32[4,8,2,4096]{3,2,1,0:T(2,128)S(1)} %fusion.9) | data formatting | bytes 2097152 | tf_op jit(solution)/shard_map/reshape | solution.py:37
  17.1 2.0 %convolution_bitcast_fusion = f32[4,8,2,64,64]{4,3,1,0,2:T(8,128)S(1)} fusion(f32[4,8,2,64,64,1]{4,3,2,1,0,5:T(8,128)S(1)} %reshape.262, f32[1,64,2,64]{1,3,0,2:T(8,128)S(1)} %get-tuple-element.29, f32[1,64,2,64]{1,3,0,2:T(8,128)S(1)} %get-tuple-element.28), kind=kOutput, calls=%fused_computation.7 | convolution fusion | flops 402669568 | bytes 2162688 | tf_op jit(solution)/shard_map/sfcxy,cxdk->sfdky/dot_general | solution.py:39
  19.1 0.4 multiply_add_fusion
  19.5 3.1 %fusion.6 = bf16[4,2,8,64,64]{4,3,2,0,1:T(8,128)(2,1)S(1)} fusion(f32[1,64,2,64]{1,3,0,2:T(8,128)S(1)} %get-tuple-element.29, f32[1,64,2,64]{1,3,0,2:T(8,128)S(1)} %get-tuple-element.28, f32[4,8,1,64,64]{4,3,1,0,2:T(8,128)S(1)} %get-tuple-element.15, f32[4,8,1,64,64]{4,3,1,0,2:T(8,128)S(1)} %get-tuple-element.14), kind=kOutput, calls=%fused_computation.8 | convolution fusion | flops 403456000 | bytes 1638400 | tf_op jit(solution)/shard_map/sfcky,cydz->sdfzk/dot_general | solution.py:49
  22.7 0.5 convert_element_type.72
  23.1 0.2 copy.22
  23.4 0.8 %gather_fusion = bf16[32,4,2,8,128]{4,3,2,1,0:T(8,128)(2,1)S(1)} fusion(bf16[4,2,8,32,128]{4,2,3,1,0:T(8,128)(2,1)S(1)} %copy.22, s32[1024]{0:T(1024)S(1)} %pad_clamp_fusion), kind=kCustom, calls=%fused_computation | custom fusion | bytes 1048704 | tf_op jit(solution)/shard_map/jit(_take)/gather | solution.py:283
  24.1 0.1 select_bitcast_fusion
  24.3 1.3 %copy.23 = bf16[32,8,4,2,128]{4,3,2,1,0:T(2,128)(2,1)} copy(bf16[32,8,4,2,128]{4,1,3,2,0:T(8,128)(2,1)S(1)} %select_bitcast_fusion) | data formatting | bytes 1048576 | tf_op jit(solution)/shard_map/jit(_take)/select_n | solution.py:283
  25.6 25.3 %exchange.1.g_ref = bf16[2,2,4,8,64,128]{5,4,3,2,1,0:T(8,128)(2,1)} custom-call(bf16[4,8,64,128]{3,2,1,0:T(8,128)(2,1)} %bitcast.69), custom_call_target="tpu_custom_call" | custom-call | tf_op jit(solution)/shard_map/exchange/pallas_call | solution.py:136
  50.9 17.8 %products.1 = (f32[8,2,16,64]{3,2,1,0:T(8,128)}, f32[4000,1024]{1,0:T(8,128)}) custom-call(s32[2]{0:T(128)} %pad_add_fusion.place_ref, bf16[10,50,64]{2,1,0:T(8,128)(2,1)} %convert_element_type.64.w_ref, bf16[64,512]{1,0:T(8,128)(2,1)} %fusion.20.col_ref, bf16[2,2,4,8,64,128]{5,4,3,2,1,0:T(8,128)(2,1)} %exchange.1.g_ref), custom_call_target="tpu_custom_call" | custom-call | tf_op jit(solution)/shard_map/products/pallas_call | solution.py:242
  (6 shorter events, 0.1 us)
Async XLA Ops:
  0.6 2.8 %copy-start = (s32[500,32]{0,1:T(8,128)S(1)}, s32[500,32]{0,1:T(8,128)}, u32[]{:S(2)}) copy-start(s32[500,32]{0,1:T(8,128)} %param.8) | copy-start | bytes 192004
  0.6 7.4 %copy-start.1 = (bf16[1,4,1,19,2,4096]{5,4,3,2,1,0:T(2,128)(2,1)S(1)}, bf16[1,4,1,19,2,4096]{5,4,3,2,1,0:T(2,128)(2,1)}, u32[]{:S(2)}) copy-start(bf16[1,4,1,19,2,4096]{5,4,3,2,1,0:T(2,128)(2,1)} %param.5) | copy-start | bytes 3735556

commit v2 on v1

--- a/solution.py
+++ b/solution.py
@@ -36,7 +36,7 @@
     stations = samples.shape[0]
     shaped = filtered.reshape(stations, frames, 2, ROOT, ROOT)
     matrix = fourier_segment(ROOT)
-    segment_one = jnp.einsum("sfcxy,cxdk->sfdky", shaped, matrix, precision=lax.Precision.HIGHEST)
+    segment_one = jnp.einsum("sfcxy,cxdk->sfdky", shaped, matrix, precision=lax.Precision.DEFAULT)
     counter = jnp.arange(ROOT, dtype=jnp.int32)
     twiddle = (counter[:, None] * counter[None, :]).astype(jnp.float32) * (
         2.0 * math.pi / (ROOT * ROOT)
@@ -46,7 +46,7 @@
     turned_real = segment_one[:, :, 0] * twiddle_cos + segment_one[:, :, 1] * twiddle_sin
     turned_imag = segment_one[:, :, 1] * twiddle_cos - segment_one[:, :, 0] * twiddle_sin
     turned = jnp.stack([turned_real, turned_imag], axis=2)
-    segment_two = jnp.einsum("sfcky,cydz->sdfzk", turned, matrix, precision=lax.Precision.HIGHEST)
+    segment_two = jnp.einsum("sfcky,cydz->sdfzk", turned, matrix, precision=lax.Precision.DEFAULT)
     return (segment_two.reshape(stations, 2, frames, ROOT * ROOT) * (1.0 / ROOT)).astype(
         jnp.bfloat16
     )
@@ -193,7 +193,9 @@
         def station(i):
             return lax.div(i, pair) * stations + lax.rem(lax.div(i, 2), stations)
 
-        left = (station(iota((own_count, m), 1)) == iota((own_count, m), 0)).astype(jnp.float32)
+        lr = iota((2 * groups * own_count, 2 * groups * m), 0)
+        lc = iota((2 * groups * own_count, 2 * groups * m), 1)
+        left = (lax.div(lc, m) * own_count + station(lax.rem(lc, m)) == lr).astype(jnp.float32)
         inputs = sections * 2 * own_count
         for p in range(2):
             q = jnp.where(pol == 0, p, 1 - p)
@@ -210,13 +212,13 @@
                     raw = raw + lax.dot_general(
                         mine, theirs, (((1,), (1,)), ((), ())), preferred_element_type=jnp.float32
                     )
-                for mask in (re_mask, im_mask):
-                    halves.append(
-                        jnp.dot(left, raw * mask, precision=lax.Precision.HIGHEST, preferred_element_type=jnp.float32)
-                    )
-            total = jnp.dot(
+                halves += [raw * re_mask, raw * im_mask]
+            columns = jnp.dot(
                 jnp.concatenate(halves, axis=0), right,
                 precision=lax.Precision.HIGHEST, preferred_element_type=jnp.float32,
+            )
+            total = jnp.dot(
+                left, columns, precision=lax.Precision.HIGHEST, preferred_element_type=jnp.float32
             ).reshape(groups, 2, own_count, inputs)
             if p == 0:
                 vis_ref[...] = total

time: 69.2 us -> 64 us (0.925)
  matrix products: 5.09 us -> 1.18 us
    dot_general x2, matrix products: 5.09 us -> 1.18 us  [the longest x1 0.71 us: channelise(): jnp.einsum('sfcky,cydz->sdfzk', turned, matrix, precision=lax.Precision.D...]
where the time goes in v2:
time: 64 us; the launch traced here: 63.6 us
  Pallas kernels  42.8 us (67%)
  other arithmetic  11.4 us (18%)
  local copies, waits for them, and re-layouts  7.38 us (12%)
  matrix products  1.18 us (2%)
  between operations  0.8 us (1%)
    pallas_call x1, Pallas kernels, exchange(): pl.pallas_call(functools.partial(exchange_kernel, owners, sections), out_...  25.3 us
    pallas_call x1, Pallas kernels, products(): pl.pallas_call(functools.partial(product_kernel, frames, stations, mean_f...  17.6 us
    add x1, other arithmetic, channelise(): filtered + filter_taps[tap_index] * samples[:, tap_index:tap_index + frames]  6.49 us
    slice x1, local copies, waits for them, and re-layouts, channelise(): filtered = filter_taps[0] * samples[:, 0:frames]  2.1 us
    select_n x1, local copies, waits for them, and re-layouts, on_device(): regrouped = jnp.take(grouped, block_owner, axis=3)  1.32 us

profile of v2, /device:TPU:0, one launch (start us, length us, event | category | flops | bytes accessed | tf_op | source)
XLA Modules:
  0.0 63.6 jit_solution(8437191882613704195)
XLA Ops:
  0.6 0.0 copy-start
  0.6 0.0 copy-start.1
  0.7 0.7 %pad_add_fusion.place_ref = s32[2]{0:T(128)} fusion(s32[1]{0:T(128)} %bitcast.1, s32[1]{0:T(128)} %bitcast), kind=kLoop, calls=%fused_computation.91 | loop fusion | flops 2 | bytes 16 | tf_op jit(solution)/shard_map/stack | solution.py:242
  1.3 0.7 %compare_and_fusion = pred[32]{0:T(512)(128)(4,1)S(1)} fusion(s32[32]{0:T(128)} %param.9), kind=kLoop, calls=%fused_computation.90 | loop fusion | flops 192 | bytes 160 | tf_op jit(solution)/shard_map/jit(_take)/and | solution.py:285
  2.0 0.7 %compare_select_fusion = s32[32]{0:T(128)S(1)} fusion(s32[32]{0:T(128)} %param.9), kind=kLoop, calls=%fused_computation.80 | loop fusion | flops 96 | bytes 256 | tf_op jit(solution)/shard_map/jit(_take)/jit(_where)/select_n | solution.py:285
  2.6 0.8 %slice_bitcast_fusion.1 = (f32[16]{0:T(128)S(1)}, f32[16]{0:T(128)S(1)}) fusion(f32[2,16]{1,0:T(2,128)} %param.7), kind=kLoop, calls=%fused_computation.93 | loop fusion | bytes 256 | tf_op jit(solution)/shard_map/squeeze | solution.py:271
  3.4 0.1 fusion.31
  3.6 0.0 copy-done
  3.6 0.1 constant_dynamic-slice_fusion
  3.7 0.3 select_reduce_fusion
  4.0 0.2 fusion.29
  4.2 0.1 copy.19
  4.3 0.9 %convert_element_type.64.w_ref = bf16[10,50,64]{2,1,0:T(8,128)(2,1)} reshape(bf16[250,2,64]{2,1,0:T(2,128)(2,1)S(1)} %copy.19) | data formatting | bytes 128000 | tf_op jit(solution)/shard_map/convert_element_type | solution.py:275
  5.2 0.6 fusion.20.col_ref
  5.8 0.1 fusion.24
  6.0 2.1 %fusion.47 = (f32[1,4096]{1,0:T(1,128)S(1)}, f32[1,4096]{1,0:T(1,128)S(1)}, f32[1,4096]{1,0:T(1,128)S(1)}, f32[1,4096]{1,0:T(1,128)S(1)}, f32[1,4096]{1,0:T(1,12...) fusion(f32[12,4096]{1,0:T(8,128)} %param.6), kind=kLoop, calls=%fused_computation.97 | loop fusion | bytes 393216 | tf_op jit(solution)/shard_map/slice | solution.py:33
  8.1 0.0 copy-done.1
  8.1 1.1 %bitcast_convert_fusion = f32[4,19,2,4096]{3,2,1,0:T(2,128)S(1)} fusion(bf16[1,4,1,19,2,4096]{5,4,3,2,1,0:T(2,128)(2,1)S(1)} %copy-done.1), kind=kLoop, calls=%fused_computation.9 | loop fusion | flops 622592 | bytes 3735552 | tf_op jit(solution)/shard_map/convert_element_type | solution.py:30
  9.1 6.5 %fusion.9 = bf16[4,8,2,4096]{3,2,1,0:T(2,128)(2,1)S(1)} fusion(f32[4,19,2,4096]{3,2,1,0:T(2,128)S(1)} %bitcast_convert_fusion, f32[4096]{0:T(1024)S(1)} %bitcast.80, f32[4096]{0:T(1024)S(1)} %bitcast.81, f32[4096]{0:T(1024)S(1)} %bitcast.71, f32[4096]{0:T(1024)S(1)} %bitcast.72, f32[4096]{0:T(1024)S(1)} %bitcast.73, f32[4096]{0:T(1024)S(1)} %bitcast.74, ...), kind=kLoop, calls=%fused_computation.11 | loop fusion | flops 6291456 | bytes 13303808 | tf_op jit(solution)/shard_map/add | solution.py:35
  15.6 0.7 %reshape.262 = bf16[4,8,2,64,64,1]{4,3,2,1,0,5:T(8,128)(2,1)S(1)} reshape(bf16[4,8,2,4096]{3,2,1,0:T(2,128)(2,1)S(1)} %fusion.9) | data formatting | bytes 1048576 | tf_op jit(solution)/shard_map/reshape | solution.py:37
  16.3 0.5 convolution_bitcast_fusion
  16.8 0.3 multiply_add_fusion
  17.1 0.7 %fusion.6 = bf16[4,2,8,64,64]{4,3,2,0,1:T(8,128)(2,1)S(1)} fusion(bf16[1,64,2,64]{1,3,0,2:T(8,128)(2,1)S(1)} %get-tuple-element.31, bf16[1,64,2,64]{1,3,0,2:T(8,128)(2,1)S(1)} %get-tuple-element.30, bf16[4,8,1,64,64]{4,3,1,0,2:T(8,128)(2,1)S(1)} %get-tuple-element.15, bf16[4,8,1,64,64]{4,3,1,0,2:T(8,128)(2,1)S(1)} %get-tuple-element.14), kind=kOutput, calls=%fused_computation.8 | convolution fusion | flops 67960832 | bytes 1081344 | tf_op jit(solution)/shard_map/sfcky,cydz->sdfzk/dot_general | solution.py:49
  17.8 0.5 convert_element_type.72
  18.3 0.2 copy.22
  18.5 0.8 %gather_fusion = bf16[32,4,2,8,128]{4,3,2,1,0:T(8,128)(2,1)S(1)} fusion(bf16[4,2,8,32,128]{4,2,3,1,0:T(8,128)(2,1)S(1)} %copy.22, s32[1024]{0:T(1024)S(1)} %pad_clamp_fusion), kind=kCustom, calls=%fused_computation | custom fusion | bytes 1048704 | tf_op jit(solution)/shard_map/jit(_take)/gather | solution.py:285
  19.3 0.1 select_bitcast_fusion
  19.4 1.3 %copy.23 = bf16[32,8,4,2,128]{4,3,2,1,0:T(2,128)(2,1)} copy(bf16[32,8,4,2,128]{4,1,3,2,0:T(8,128)(2,1)S(1)} %select_bitcast_fusion) | data formatting | bytes 1048576 | tf_op jit(solution)/shard_map/jit(_take)/select_n | solution.py:285
  20.7 25.3 %exchange.1.g_ref = bf16[2,2,4,8,64,128]{5,4,3,2,1,0:T(8,128)(2,1)} custom-call(bf16[4,8,64,128]{3,2,1,0:T(8,128)(2,1)} %bitcast.69), custom_call_target="tpu_custom_call" | custom-call | tf_op jit(solution)/shard_map/exchange/pallas_call | solution.py:136
  46.0 17.6 %products.1 = (f32[8,2,16,64]{3,2,1,0:T(8,128)}, f32[4000,1024]{1,0:T(8,128)}) custom-call(s32[2]{0:T(128)} %pad_add_fusion.place_ref, bf16[10,50,64]{2,1,0:T(8,128)(2,1)} %convert_element_type.64.w_ref, bf16[64,512]{1,0:T(8,128)(2,1)} %fusion.20.col_ref, bf16[2,2,4,8,64,128]{5,4,3,2,1,0:T(8,128)(2,1)} %exchange.1.g_ref), custom_call_target="tpu_custom_call" | custom-call | tf_op jit(solution)/shard_map/products/pallas_call | solution.py:244
  (6 shorter events, 0.1 us)
Async XLA Ops:
  0.6 2.9 %copy-start = (s32[500,32]{0,1:T(8,128)S(1)}, s32[500,32]{0,1:T(8,128)}, u32[]{:S(2)}) copy-start(s32[500,32]{0,1:T(8,128)} %param.8) | copy-start | bytes 192004
  0.6 7.4 %copy-start.1 = (bf16[1,4,1,19,2,4096]{5,4,3,2,1,0:T(2,128)(2,1)S(1)}, bf16[1,4,1,19,2,4096]{5,4,3,2,1,0:T(2,128)(2,1)}, u32[]{:S(2)}) copy-start(bf16[1,4,1,19,2,4096]{5,4,3,2,1,0:T(2,128)(2,1)} %param.5) | copy-start | bytes 3735556

commit v3 on v1

--- a/solution.py
+++ b/solution.py
@@ -36,7 +36,7 @@
     stations = samples.shape[0]
     shaped = filtered.reshape(stations, frames, 2, ROOT, ROOT)
     matrix = fourier_segment(ROOT)
-    segment_one = jnp.einsum("sfcxy,cxdk->sfdky", shaped, matrix, precision=lax.Precision.HIGHEST)
+    segment_one = jnp.einsum("sfcxy,cxdk->sfdky", shaped, matrix, precision=lax.Precision.DEFAULT)
     counter = jnp.arange(ROOT, dtype=jnp.int32)
     twiddle = (counter[:, None] * counter[None, :]).astype(jnp.float32) * (
         2.0 * math.pi / (ROOT * ROOT)
@@ -46,7 +46,7 @@
     turned_real = segment_one[:, :, 0] * twiddle_cos + segment_one[:, :, 1] * twiddle_sin
     turned_imag = segment_one[:, :, 1] * twiddle_cos - segment_one[:, :, 0] * twiddle_sin
     turned = jnp.stack([turned_real, turned_imag], axis=2)
-    segment_two = jnp.einsum("sfcky,cydz->sdfzk", turned, matrix, precision=lax.Precision.HIGHEST)
+    segment_two = jnp.einsum("sfcky,cydz->sdfzk", turned, matrix, precision=lax.Precision.DEFAULT)
     return (segment_two.reshape(stations, 2, frames, ROOT * ROOT) * (1.0 / ROOT)).astype(
         jnp.bfloat16
     )

time: 69.2 us -> 64.1 us (0.926)
  matrix products: 5.09 us -> 1.17 us
    dot_general x2, matrix products: 5.09 us -> 1.17 us  [the longest x1 0.69 us: channelise(): jnp.einsum('sfcky,cydz->sdfzk', turned, matrix, precision=lax.Precision.D...]
where the time goes in v3:
time: 64.1 us; the launch traced here: 63.6 us
  Pallas kernels  43.1 us (67%)
  other arithmetic  11.2 us (17%)
  local copies, waits for them, and re-layouts  7.39 us (12%)
  matrix products  1.17 us (2%)
  between operations  0.8 us (1%)
    pallas_call x1, Pallas kernels, exchange(): pl.pallas_call(functools.partial(exchange_kernel, owners, sections), out_...  25.3 us
    pallas_call x1, Pallas kernels, products(): pl.pallas_call(functools.partial(product_kernel, frames, stations, mean_f...  17.8 us
    add x1, other arithmetic, channelise(): filtered + filter_taps[tap_index] * samples[:, tap_index:tap_index + frames]  6.31 us
    slice x1, local copies, waits for them, and re-layouts, channelise(): filtered = filter_taps[0] * samples[:, 0:frames]  2.1 us
    select_n x1, local copies, waits for them, and re-layouts, on_device(): regrouped = jnp.take(grouped, block_owner, axis=3)  1.32 us

profile of v3, /device:TPU:0, one launch (start us, length us, event | category | flops | bytes accessed | tf_op | source)
XLA Modules:
  0.0 63.6 jit_solution(12336027734113003722)
XLA Ops:
  0.6 0.0 copy-start
  0.6 0.0 copy-start.1
  0.7 0.7 %pad_add_fusion.place_ref = s32[2]{0:T(128)} fusion(s32[1]{0:T(128)} %bitcast.1, s32[1]{0:T(128)} %bitcast), kind=kLoop, calls=%fused_computation.91 | loop fusion | flops 2 | bytes 16 | tf_op jit(solution)/shard_map/stack | solution.py:240
  1.3 0.7 %compare_and_fusion = pred[32]{0:T(512)(128)(4,1)S(1)} fusion(s32[32]{0:T(128)} %param.9), kind=kLoop, calls=%fused_computation.90 | loop fusion | flops 192 | bytes 160 | tf_op jit(solution)/shard_map/jit(_take)/and | solution.py:283
  2.0 0.7 %compare_select_fusion = s32[32]{0:T(128)S(1)} fusion(s32[32]{0:T(128)} %param.9), kind=kLoop, calls=%fused_computation.80 | loop fusion | flops 96 | bytes 256 | tf_op jit(solution)/shard_map/jit(_take)/jit(_where)/select_n | solution.py:283
  2.6 0.8 %slice_bitcast_fusion.1 = (f32[16]{0:T(128)S(1)}, f32[16]{0:T(128)S(1)}) fusion(f32[2,16]{1,0:T(2,128)} %param.7), kind=kLoop, calls=%fused_computation.93 | loop fusion | bytes 256 | tf_op jit(solution)/shard_map/squeeze | solution.py:269
  3.4 0.1 fusion.31
  3.6 0.0 copy-done
  3.6 0.1 constant_dynamic-slice_fusion
  3.7 0.3 select_reduce_fusion
  4.0 0.2 fusion.29
  4.2 0.1 copy.19
  4.3 0.9 %convert_element_type.64.w_ref = bf16[10,50,64]{2,1,0:T(8,128)(2,1)} reshape(bf16[250,2,64]{2,1,0:T(2,128)(2,1)S(1)} %copy.19) | data formatting | bytes 128000 | tf_op jit(solution)/shard_map/convert_element_type | solution.py:273
  5.2 0.6 fusion.20.col_ref
  5.8 0.1 fusion.24
  6.0 2.1 %fusion.47 = (f32[1,4096]{1,0:T(1,128)S(1)}, f32[1,4096]{1,0:T(1,128)S(1)}, f32[1,4096]{1,0:T(1,128)S(1)}, f32[1,4096]{1,0:T(1,128)S(1)}, f32[1,4096]{1,0:T(1,12...) fusion(f32[12,4096]{1,0:T(8,128)} %param.6), kind=kLoop, calls=%fused_computation.97 | loop fusion | bytes 393216 | tf_op jit(solution)/shard_map/slice | solution.py:33
  8.1 0.0 copy-done.1
  8.1 1.1 %bitcast_convert_fusion = f32[4,19,2,4096]{3,2,1,0:T(2,128)S(1)} fusion(bf16[1,4,1,19,2,4096]{5,4,3,2,1,0:T(2,128)(2,1)S(1)} %copy-done.1), kind=kLoop, calls=%fused_computation.9 | loop fusion | flops 622592 | bytes 3735552 | tf_op jit(solution)/shard_map/convert_element_type | solution.py:30
  9.1 6.3 %fusion.9 = bf16[4,8,2,4096]{3,2,1,0:T(2,128)(2,1)S(1)} fusion(f32[4,19,2,4096]{3,2,1,0:T(2,128)S(1)} %bitcast_convert_fusion, f32[4096]{0:T(1024)S(1)} %bitcast.80, f32[4096]{0:T(1024)S(1)} %bitcast.81, f32[4096]{0:T(1024)S(1)} %bitcast.71, f32[4096]{0:T(1024)S(1)} %bitcast.72, f32[4096]{0:T(1024)S(1)} %bitcast.73, f32[4096]{0:T(1024)S(1)} %bitcast.74, ...), kind=kLoop, calls=%fused_computation.11 | loop fusion | flops 6291456 | bytes 13303808 | tf_op jit(solution)/shard_map/add | solution.py:35
  15.5 0.7 %reshape.262 = bf16[4,8,2,64,64,1]{4,3,2,1,0,5:T(8,128)(2,1)S(1)} reshape(bf16[4,8,2,4096]{3,2,1,0:T(2,128)(2,1)S(1)} %fusion.9) | data formatting | bytes 1048576 | tf_op jit(solution)/shard_map/reshape | solution.py:37
  16.1 0.5 convolution_bitcast_fusion
  16.6 0.3 multiply_add_fusion
  16.9 0.7 %fusion.6 = bf16[4,2,8,64,64]{4,3,2,0,1:T(8,128)(2,1)S(1)} fusion(bf16[1,64,2,64]{1,3,0,2:T(8,128)(2,1)S(1)} %get-tuple-element.31, bf16[1,64,2,64]{1,3,0,2:T(8,128)(2,1)S(1)} %get-tuple-element.30, bf16[4,8,1,64,64]{4,3,1,0,2:T(8,128)(2,1)S(1)} %get-tuple-element.15, bf16[4,8,1,64,64]{4,3,1,0,2:T(8,128)(2,1)S(1)} %get-tuple-element.14), kind=kOutput, calls=%fused_computation.8 | convolution fusion | flops 67960832 | bytes 1081344 | tf_op jit(solution)/shard_map/sfcky,cydz->sdfzk/dot_general | solution.py:49
  17.6 0.5 convert_element_type.72
  18.1 0.2 copy.22
  18.3 0.8 %gather_fusion = bf16[32,4,2,8,128]{4,3,2,1,0:T(8,128)(2,1)S(1)} fusion(bf16[4,2,8,32,128]{4,2,3,1,0:T(8,128)(2,1)S(1)} %copy.22, s32[1024]{0:T(1024)S(1)} %pad_clamp_fusion), kind=kCustom, calls=%fused_computation | custom fusion | bytes 1048704 | tf_op jit(solution)/shard_map/jit(_take)/gather | solution.py:283
  19.1 0.1 select_bitcast_fusion
  19.2 1.3 %copy.23 = bf16[32,8,4,2,128]{4,3,2,1,0:T(2,128)(2,1)} copy(bf16[32,8,4,2,128]{4,1,3,2,0:T(8,128)(2,1)S(1)} %select_bitcast_fusion) | data formatting | bytes 1048576 | tf_op jit(solution)/shard_map/jit(_take)/select_n | solution.py:283
  20.5 25.3 %exchange.1.g_ref = bf16[2,2,4,8,64,128]{5,4,3,2,1,0:T(8,128)(2,1)} custom-call(bf16[4,8,64,128]{3,2,1,0:T(8,128)(2,1)} %bitcast.69), custom_call_target="tpu_custom_call" | custom-call | tf_op jit(solution)/shard_map/exchange/pallas_call | solution.py:136
  45.8 17.8 %products.1 = (f32[8,2,16,64]{3,2,1,0:T(8,128)}, f32[4000,1024]{1,0:T(8,128)}) custom-call(s32[2]{0:T(128)} %pad_add_fusion.place_ref, bf16[10,50,64]{2,1,0:T(8,128)(2,1)} %convert_element_type.64.w_ref, bf16[64,512]{1,0:T(8,128)(2,1)} %fusion.20.col_ref, bf16[2,2,4,8,64,128]{5,4,3,2,1,0:T(8,128)(2,1)} %exchange.1.g_ref), custom_call_target="tpu_custom_call" | custom-call | tf_op jit(solution)/shard_map/products/pallas_call | solution.py:242
  (6 shorter events, 0.1 us)
Async XLA Ops:
  0.6 2.9 %copy-start = (s32[500,32]{0,1:T(8,128)S(1)}, s32[500,32]{0,1:T(8,128)}, u32[]{:S(2)}) copy-start(s32[500,32]{0,1:T(8,128)} %param.8) | copy-start | bytes 192004
  0.6 7.4 %copy-start.1 = (bf16[1,4,1,19,2,4096]{5,4,3,2,1,0:T(2,128)(2,1)S(1)}, bf16[1,4,1,19,2,4096]{5,4,3,2,1,0:T(2,128)(2,1)}, u32[]{:S(2)}) copy-start(bf16[1,4,1,19,2,4096]{5,4,3,2,1,0:T(2,128)(2,1)} %param.5) | copy-start | bytes 3735556

commit v4 on v3

--- a/solution.py
+++ b/solution.py
@@ -3,6 +3,7 @@
 
 import jax
 import jax.numpy as jnp
+import numpy as np
 from jax import lax
 from jax.experimental import pallas as pl
 from jax.experimental.pallas import tpu as pltpu
@@ -15,15 +16,15 @@
 
 
 def fourier_segment(length):
-    counter = jnp.arange(length, dtype=jnp.int32)
-    phase = (counter[:, None] * counter[None, :] % length).astype(jnp.float32) * (
+    counter = np.arange(length, dtype=np.int32)
+    phase = (counter[:, None] * counter[None, :] % length) * (
         2.0 * math.pi / length
     )
-    cosine = jnp.cos(phase)
-    sine = jnp.sin(phase)
-    upper_half = jnp.stack([cosine, -sine], axis=1)
-    lower_half = jnp.stack([sine, cosine], axis=1)
-    return jnp.stack([upper_half, lower_half], axis=0)
+    cosine = np.cos(phase)
+    sine = np.sin(phase)
+    upper_half = np.stack([cosine, -sine], axis=1)
+    lower_half = np.stack([sine, cosine], axis=1)
+    return np.stack([upper_half, lower_half], axis=0).astype(np.float32)
 
 
 def channelise(voltages, filter_taps):
@@ -37,12 +38,10 @@
     shaped = filtered.reshape(stations, frames, 2, ROOT, ROOT)
     matrix = fourier_segment(ROOT)
     segment_one = jnp.einsum("sfcxy,cxdk->sfdky", shaped, matrix, precision=lax.Precision.DEFAULT)
-    counter = jnp.arange(ROOT, dtype=jnp.int32)
-    twiddle = (counter[:, None] * counter[None, :]).astype(jnp.float32) * (
-        2.0 * math.pi / (ROOT * ROOT)
-    )
-    twiddle_cos = jnp.cos(twiddle)
-    twiddle_sin = jnp.sin(twiddle)
+    counter = np.arange(ROOT)
+    twiddle = counter[:, None] * counter[None, :] * (2.0 * math.pi / (ROOT * ROOT))
+    twiddle_cos = np.cos(twiddle).astype(np.float32)
+    twiddle_sin = np.sin(twiddle).astype(np.float32)
     turned_real = segment_one[:, :, 0] * twiddle_cos + segment_one[:, :, 1] * twiddle_sin
     turned_imag = segment_one[:, :, 1] * twiddle_cos - segment_one[:, :, 0] * twiddle_sin
     turned = jnp.stack([turned_real, turned_imag], axis=2)
@@ -136,8 +135,8 @@
     return pl.pallas_call(
         functools.partial(exchange_kernel, owners, sections),
         out_shape=jax.ShapeDtypeStruct((2, sections) + blocks.shape, blocks.dtype),
-        in_specs=[pl.BlockSpec(memory_space=pl.ANY)],
-        out_specs=pl.BlockSpec(memory_space=pl.ANY),
+        in_specs=[pl.BlockSpec(memory_space=pltpu.VMEM)],
+        out_specs=pl.BlockSpec(memory_space=pltpu.VMEM),
         scratch_shapes=[
             pltpu.SemaphoreType.DMA((owners,)),
             pltpu.SemaphoreType.DMA((owners,)),

time: 64.1 us -> 64.9 us (1.012)
  Pallas kernels: 43.1 us -> 43.8 us
  local copies, waits for them, and re-layouts: 7.39 us -> 8.06 us
    pallas_call x1, Pallas kernels: 25.3 us -> 26 us  [exchange(): pl.pallas_call(functools.partial(exchange_kernel, owners, sections), out_...]
    convert_element_type x2 -> x3, local copies, waits for them, and re-layouts: 0.69 us -> 1.35 us  [channelise(): (segment_two.reshape(stations, 2, frames, ROOT * ROOT) * (1.0 / ROOT)).as...]
where the time goes in v4:
time: 64.9 us; the launch traced here: 64.4 us
  Pallas kernels  43.8 us (67%)
  other arithmetic  10.7 us (16%)
  local copies, waits for them, and re-layouts  8.06 us (12%)
  matrix products  0.95 us (1%)
  between operations  0.85 us (1%)
    pallas_call x1, Pallas kernels, exchange(): pl.pallas_call(functools.partial(exchange_kernel, owners, sections), out_...  26 us
    pallas_call x1, Pallas kernels, products(): pl.pallas_call(functools.partial(product_kernel, frames, stations, mean_f...  17.8 us
    add x1, other arithmetic, channelise(): filtered + filter_taps[tap_index] * samples[:, tap_index:tap_index + frames]  6.31 us
    slice x1, local copies, waits for them, and re-layouts, channelise(): filtered = filter_taps[0] * samples[:, 0:frames]  2.09 us
    convert_element_type x3, local copies, waits for them, and re-layouts, channelise(): (segment_two.reshape(stations, 2, frames, ROOT * ROOT) * (1.0 / ROOT)).as...  1.35 us
    select_n x1, local copies, waits for them, and re-layouts, on_device(): regrouped = jnp.take(grouped, block_owner, axis=3)  1.32 us

profile of v4, /device:TPU:0, one launch (start us, length us, event | category | flops | bytes accessed | tf_op | source)
XLA Modules:
  0.0 64.4 jit_solution(823426585594755753)
XLA Ops:
  0.6 0.0 copy-start
  0.6 0.0 copy-start.1
  0.7 0.7 %pad_add_fusion.place_ref = s32[2]{0:T(128)} fusion(s32[1]{0:T(128)} %bitcast.1, s32[1]{0:T(128)} %bitcast), kind=kLoop, calls=%fused_computation.75 | loop fusion | flops 2 | bytes 16 | tf_op jit(solution)/shard_map/stack | solution.py:239
  1.3 0.7 %compare_and_fusion = pred[32]{0:T(512)(128)(4,1)S(1)} fusion(s32[32]{0:T(128)} %param.13), kind=kLoop, calls=%fused_computation.74 | loop fusion | flops 192 | bytes 160 | tf_op jit(solution)/shard_map/jit(_take)/and | solution.py:282
  2.0 0.7 %compare_select_fusion = s32[32]{0:T(128)S(1)} fusion(s32[32]{0:T(128)} %param.13), kind=kLoop, calls=%fused_computation.64 | loop fusion | flops 96 | bytes 256 | tf_op jit(solution)/shard_map/jit(_take)/jit(_where)/select_n | solution.py:282
  2.6 0.8 %slice_bitcast_fusion.1 = (f32[16]{0:T(128)S(1)}, f32[16]{0:T(128)S(1)}) fusion(f32[2,16]{1,0:T(2,128)} %param.11), kind=kLoop, calls=%fused_computation.77 | loop fusion | bytes 256 | tf_op jit(solution)/shard_map/squeeze | solution.py:268
  3.4 0.0 copy-done
  3.4 0.1 constant_dynamic-slice_fusion
  3.5 0.3 select_reduce_fusion
  3.9 0.1 copy.24
  4.0 0.9 %convert_element_type.24.w_ref = bf16[10,50,64]{2,1,0:T(8,128)(2,1)} reshape(bf16[250,2,64]{2,1,0:T(2,128)(2,1)S(1)} %copy.24) | data formatting | bytes 128000 | tf_op jit(solution)/shard_map/convert_element_type | solution.py:272
  4.9 0.6 fusion.21.col_ref
  5.5 2.1 %fusion.36 = (f32[1,4096]{1,0:T(1,128)S(1)}, f32[1,4096]{1,0:T(1,128)S(1)}, f32[1,4096]{1,0:T(1,128)S(1)}, f32[1,4096]{1,0:T(1,128)S(1)}, f32[1,4096]{1,0:T(1,12...) fusion(f32[12,4096]{1,0:T(8,128)} %param.10), kind=kLoop, calls=%fused_computation.80 | loop fusion | bytes 393216 | tf_op jit(solution)/shard_map/slice | solution.py:34
  7.6 0.0 copy-done.1
  7.6 1.1 %bitcast_convert_fusion = f32[4,19,2,4096]{3,2,1,0:T(2,128)S(1)} fusion(bf16[1,4,1,19,2,4096]{5,4,3,2,1,0:T(2,128)(2,1)S(1)} %copy-done.1), kind=kLoop, calls=%fused_computation.11 | loop fusion | flops 622592 | bytes 3735552 | tf_op jit(solution)/shard_map/convert_element_type | solution.py:31
  8.7 0.0 copy-start.2
  8.7 6.3 %fusion.10 = bf16[4,8,2,4096]{3,2,1,0:T(2,128)(2,1)S(1)} fusion(f32[4,19,2,4096]{3,2,1,0:T(2,128)S(1)} %bitcast_convert_fusion, f32[4096]{0:T(1024)S(1)} %bitcast.79, f32[4096]{0:T(1024)S(1)} %bitcast.80, f32[4096]{0:T(1024)S(1)} %bitcast.70, f32[4096]{0:T(1024)S(1)} %bitcast.71, f32[4096]{0:T(1024)S(1)} %bitcast.72, f32[4096]{0:T(1024)S(1)} %bitcast.73, ...), kind=kLoop, calls=%fused_computation.13 | loop fusion | flops 6291456 | bytes 13303808 | tf_op jit(solution)/shard_map/add | solution.py:36
  15.0 0.0 copy-start.3
  15.0 0.0 copy-start.4
  15.0 0.7 %reshape.150 = bf16[4,8,2,64,64]{4,3,2,1,0:T(8,128)(2,1)S(1)} reshape(bf16[4,8,2,4096]{3,2,1,0:T(2,128)(2,1)S(1)} %fusion.10) | data formatting | bytes 1048576 | tf_op jit(solution)/shard_map/reshape | solution.py:38
  15.7 0.0 copy-done.2
  15.7 0.5 fusion.6
  16.2 0.0 copy-done.3
  16.2 0.0 copy-done.4
  16.2 0.3 multiply_add_fusion
  16.5 0.5 fusion.9
  17.0 0.7 %copy.27 = bf16[4,2,8,64,64]{4,3,2,1,0:T(8,128)(2,1)S(1)} copy(bf16[4,2,8,64,64]{3,4,1,2,0:T(8,128)(2,1)S(1)} %fusion.9) | data formatting | bytes 1048576 | tf_op jit(solution)/shard_map/convert_element_type | solution.py:49
  17.7 0.5 convert_element_type.30
  18.1 0.2 copy.28
  18.4 0.8 %gather_fusion = bf16[32,4,2,8,128]{4,3,2,1,0:T(8,128)(2,1)S(1)} fusion(bf16[4,2,8,32,128]{4,2,3,1,0:T(8,128)(2,1)S(1)} %copy.28, s32[1024]{0:T(1024)S(1)} %pad_clamp_fusion), kind=kCustom, calls=%fused_computation | custom fusion | bytes 1048704 | tf_op jit(solution)/shard_map/jit(_take)/gather | solution.py:282
  19.2 0.1 select_bitcast_fusion
  19.3 1.3 %copy.29 = bf16[32,8,4,2,128]{4,3,2,1,0:T(2,128)(2,1)} copy(bf16[32,8,4,2,128]{4,1,3,2,0:T(8,128)(2,1)S(1)} %select_bitcast_fusion) | data formatting | bytes 1048576 | tf_op jit(solution)/shard_map/jit(_take)/select_n | solution.py:282
  20.6 26.0 %exchange.1.g_ref = bf16[2,2,4,8,64,128]{5,4,3,2,1,0:T(8,128)(2,1)} custom-call(bf16[4,8,64,128]{3,2,1,0:T(8,128)(2,1)} %bitcast.68), custom_call_target="tpu_custom_call" | custom-call | tf_op jit(solution)/shard_map/exchange/pallas_call | solution.py:135
  46.6 17.8 %products.1 = (f32[8,2,16,64]{3,2,1,0:T(8,128)}, f32[4000,1024]{1,0:T(8,128)}) custom-call(s32[2]{0:T(128)} %pad_add_fusion.place_ref, bf16[10,50,64]{2,1,0:T(8,128)(2,1)} %convert_element_type.24.w_ref, bf16[64,512]{1,0:T(8,128)(2,1)} %fusion.21.col_ref, bf16[2,2,4,8,64,128]{5,4,3,2,1,0:T(8,128)(2,1)} %exchange.1.g_ref), custom_call_target="tpu_custom_call" | custom-call | tf_op jit(solution)/shard_map/products/pallas_call | solution.py:241
  (5 shorter events, 0.1 us)
Async XLA Ops:
  0.6 2.8 %copy-start = (s32[500,32]{0,1:T(8,128)S(1)}, s32[500,32]{0,1:T(8,128)}, u32[]{:S(2)}) copy-start(s32[500,32]{0,1:T(8,128)} %param.12) | copy-start | bytes 192004
  0.6 6.9 %copy-start.1 = (bf16[1,4,1,19,2,4096]{5,4,3,2,1,0:T(2,128)(2,1)S(1)}, bf16[1,4,1,19,2,4096]{5,4,3,2,1,0:T(2,128)(2,1)}, u32[]{:S(2)}) copy-start(bf16[1,4,1,19,2,4096]{5,4,3,2,1,0:T(2,128)(2,1)} %param.9) | copy-start | bytes 3735556
  8.7 7.0 %copy-start.2 = (bf16[2,64,2,64,1,1]{3,1,0,2,5,4:T(8,128)(2,1)S(1)}, bf16[2,64,2,64,1,1]{3,1,0,2,5,4:T(8,128)(2,1)}, u32[]{:S(2)}) copy-start(bf16[2,64,2,64,1,1]{3,1,0,2,5,4:T(8,128)(2,1)} %constant.174) | copy-start | bytes 98308
  15.0 1.2 %copy-start.3 = (f32[64,64]{0,1:T(8,128)S(1)}, f32[64,64]{0,1:T(8,128)}, u32[]{:S(2)}) copy-start(f32[64,64]{0,1:T(8,128)} %constant.95.clone) | copy-start | bytes 49156
  15.0 1.2 %copy-start.4 = (f32[64,64]{0,1:T(8,128)S(1)}, f32[64,64]{0,1:T(8,128)}, u32[]{:S(2)}) copy-start(f32[64,64]{0,1:T(8,128)} %constant.94.clone) | copy-start | bytes 49156

commit v5 on v4

--- a/solution.py
+++ b/solution.py
@@ -135,8 +135,8 @@
     return pl.pallas_call(
         functools.partial(exchange_kernel, owners, sections),
         out_shape=jax.ShapeDtypeStruct((2, sections) + blocks.shape, blocks.dtype),
-        in_specs=[pl.BlockSpec(memory_space=pltpu.VMEM)],
-        out_specs=pl.BlockSpec(memory_space=pltpu.VMEM),
+        in_specs=[pl.BlockSpec(memory_space=pl.ANY)],
+        out_specs=pl.BlockSpec(memory_space=pl.ANY),
         scratch_shapes=[
             pltpu.SemaphoreType.DMA((owners,)),
             pltpu.SemaphoreType.DMA((owners,)),
@@ -263,10 +263,14 @@
 
 
 def beam_weights(indices, beam_table, factor):
-    levels = jnp.arange(beam_table.shape[1], dtype=jnp.int32)
-    selected = indices[..., None] == levels
-    w_real = jnp.sum(jnp.where(selected, beam_table[0], 0.0), axis=-1) * factor
-    w_imag = jnp.sum(jnp.where(selected, beam_table[1], 0.0), axis=-1) * factor
+    w_real = jnp.zeros(indices.shape, jnp.float32)
+    w_imag = w_real
+    for level in range(beam_table.shape[1]):
+        selected = indices == level
+        w_real = jnp.where(selected, beam_table[0, level], w_real)
+        w_imag = jnp.where(selected, beam_table[1, level], w_imag)
+    w_real = w_real * factor
+    w_imag = w_imag * factor
     upper_half = jnp.concatenate([w_real, -w_imag], axis=1)
     lower_half = jnp.concatenate([w_imag, w_real], axis=1)
     return jnp.stack([upper_half, lower_half], axis=1).astype(jnp.bfloat16)

time: 64.9 us -> 88.4 us (1.36)
  other arithmetic: 10.7 us -> 31.5 us
  local copies, waits for them, and re-layouts: 8.06 us -> 11.2 us
    another operation x1 -> x2, other arithmetic: 0.01 us -> 21.1 us
    slice x0 -> x2, local copies, waits for them, and re-layouts: none -> 3.96 us  [beam_weights(): w_real = jnp.where(selected, beam_table[0, level], w_real)]
where the time goes in v5:
time: 88.4 us; the launch traced here: 87.5 us
  Pallas kernels  43.1 us (49%)
  other arithmetic  31.5 us (36%)
  local copies, waits for them, and re-layouts  11.2 us (13%)
  matrix products  0.95 us (1%)
    pallas_call x1, Pallas kernels, exchange(): pl.pallas_call(functools.partial(exchange_kernel, owners, sections), out_...  25.3 us
    another operation x2, other arithmetic  21.1 us
    pallas_call x1, Pallas kernels, products(): pl.pallas_call(functools.partial(product_kernel, frames, stations, mean_f...  17.8 us
    add x1, other arithmetic, channelise(): filtered + filter_taps[tap_index] * samples[:, tap_index:tap_index + frames]  6.31 us
    slice x2, local copies, waits for them, and re-layouts, beam_weights(): w_real = jnp.where(selected, beam_table[0, level], w_real)  3.96 us
    slice x1, local copies, waits for them, and re-layouts, channelise(): filtered = filter_taps[0] * samples[:, 0:frames]  2.09 us

profile of v5, /device:TPU:0, one launch (start us, length us, event | category | flops | bytes accessed | tf_op | source)
XLA Modules:
  0.0 87.5 jit_solution(988590983576860697)
XLA Ops:
  0.6 0.0 copy-start
  0.6 0.6 pad_add_fusion.place_ref
  1.3 0.7 compare_and_fusion
  1.9 0.7 compare_select_fusion
  2.6 1.9 %fusion.38 = (f32[1,1]{1,0:T(1,128)}, f32[1,1]{1,0:T(1,128)}, f32[1,1]{1,0:T(1,128)}, f32[1,1]{1,0:T(1,128)}, f32[1,1]{1,0:T(1,128)}, /*index=5*/f32[1,1]{1,0:T(...) fusion(f32[2,16]{1,0:T(2,128)} %param.11), kind=kLoop, calls=%fused_computation.93 | loop fusion | bytes 104 | tf_op jit(solution)/shard_map/slice | solution.py:270
  4.5 2.1 %fusion.37 = (f32[1,1]{1,0:T(1,128)}, f32[1,1]{1,0:T(1,128)}, f32[1,1]{1,0:T(1,128)}, f32[1,1]{1,0:T(1,128)}, f32[1,1]{1,0:T(1,128)}, /*index=5*/f32[1,1]{1,0:T(...) fusion(f32[2,16]{1,0:T(2,128)} %param.11), kind=kLoop, calls=%fused_computation.92 | loop fusion | bytes 152 | tf_op jit(solution)/shard_map/slice | solution.py:270
  6.6 0.6 fusion.21.col_ref
  7.2 11.0 %negate_convert_fusion = (bf16[250,32]{0,1:T(8,128)(2,1)S(1)}, bf16[250,32]{0,1:T(8,128)(2,1)S(1)}, pred[250,32]{0,1:T(8,128)(4,1)S(1)}, pred[250,32]{0,1:T(8,12...) fusion(f32[]{:T(128)} %bitcast.33, f32[]{:T(128)} %bitcast.32, ...), kind=kLoop, calls=%fused_computation.43 | loop fusion | flops 288000 | bytes 192068 | tf_op jit(solution)/shard_map/convert.8
  18.2 10.1 %multiply_convert_fusion = bf16[250,32]{0,1:T(8,128)(2,1)S(1)} fusion(pred[250,32]{0,1:T(8,128)(4,1)S(1)} %get-tuple-element.27, pred[250,32]{0,1:T(8,128)(4,1)S(1)} %get-tuple-element.26, pred[250,32]{0,1:T(8,128)(4,1)S(1)} %get-tuple-element.25, pred[250,32]{0,1:T(8,128)(4,1)S(1)} %get-tuple-element.24, pred[250,32]{0,1:T(8,128)(4,1)S(1)} %get-tuple-element.23, ...), kind=kLoop, calls=%fused_computation.45 | loop fusion | flops 144000 | bytes 144064 | tf_op jit(solution)/shard_map/convert.7
  28.3 0.1 copy.15
  28.5 0.9 convert_element_type.24.w_ref
  29.3 2.1 %fusion.36 = (f32[1,4096]{1,0:T(1,128)S(1)}, f32[1,4096]{1,0:T(1,128)S(1)}, f32[1,4096]{1,0:T(1,128)S(1)}, f32[1,4096]{1,0:T(1,128)S(1)}, f32[1,4096]{1,0:T(1,12...) fusion(f32[12,4096]{1,0:T(8,128)} %param.10), kind=kLoop, calls=%fused_computation.91 | loop fusion | bytes 393216 | tf_op jit(solution)/shard_map/slice | solution.py:34
  31.4 0.0 copy-done
  31.4 1.1 %bitcast_convert_fusion = f32[4,19,2,4096]{3,2,1,0:T(2,128)S(1)} fusion(bf16[1,4,1,19,2,4096]{5,4,3,2,1,0:T(2,128)(2,1)S(1)} %copy-done), kind=kLoop, calls=%fused_computation.11 | loop fusion | flops 622592 | bytes 3735552 | tf_op jit(solution)/shard_map/convert_element_type | solution.py:31
  32.5 0.0 copy-start.1
  32.5 6.3 %fusion.10 = bf16[4,8,2,4096]{3,2,1,0:T(2,128)(2,1)S(1)} fusion(f32[4,19,2,4096]{3,2,1,0:T(2,128)S(1)} %bitcast_convert_fusion, f32[4096]{0:T(1024)S(1)} %bitcast.107, f32[4096]{0:T(1024)S(1)} %bitcast.108, f32[4096]{0:T(1024)S(1)} %bitcast.98, f32[4096]{0:T(1024)S(1)} %bitcast.99, f32[4096]{0:T(1024)S(1)} %bitcast.100, f32[4096]{0:T(1024)S(1)} %bitcast.101, ...), kind=kLoop, calls=%fused_computation.13 | loop fusion | flops 6291456 | bytes 13303808 | tf_op jit(solution)/shard_map/add | solution.py:36
  38.9 0.0 copy-start.2
  38.9 0.0 copy-start.3
  38.9 0.7 reshape.149
  39.5 0.0 copy-done.1
  39.6 0.5 fusion.6
  40.0 0.0 copy-done.2
  40.0 0.0 copy-done.3
  40.0 0.3 multiply_add_fusion
  40.4 0.5 fusion.9
  40.8 0.7 copy.18
  41.5 0.5 convert_element_type.30
  42.0 0.2 copy.19
  42.2 0.8 gather_fusion
  43.0 0.1 select_bitcast_fusion
  43.1 1.3 %copy.20 = bf16[32,8,4,2,128]{4,3,2,1,0:T(2,128)(2,1)} copy(bf16[32,8,4,2,128]{4,1,3,2,0:T(8,128)(2,1)S(1)} %select_bitcast_fusion) | data formatting | bytes 1048576 | tf_op jit(solution)/shard_map/jit(_take)/select_n | solution.py:286
  44.4 25.3 %exchange.1.g_ref = bf16[2,2,4,8,64,128]{5,4,3,2,1,0:T(8,128)(2,1)} custom-call(bf16[4,8,64,128]{3,2,1,0:T(8,128)(2,1)} %bitcast.96), custom_call_target="tpu_custom_call" | custom-call | tf_op jit(solution)/shard_map/exchange/pallas_call | solution.py:135
  69.7 17.8 %products.1 = (f32[8,2,16,64]{3,2,1,0:T(8,128)}, f32[4000,1024]{1,0:T(8,128)}) custom-call(s32[2]{0:T(128)} %pad_add_fusion.place_ref, bf16[10,50,64]{2,1,0:T(8,128)(2,1)} %convert_element_type.24.w_ref, bf16[64,512]{1,0:T(8,128)(2,1)} %fusion.21.col_ref, bf16[2,2,4,8,64,128]{5,4,3,2,1,0:T(8,128)(2,1)} %exchange.1.g_ref), custom_call_target="tpu_custom_call" | custom-call | tf_op jit(solution)/shard_map/products/pallas_call | solution.py:241
  (4 shorter events, 0.0 us)
Async XLA Ops:
  0.6 30.8 %copy-start = (bf16[1,4,1,19,2,4096]{5,4,3,2,1,0:T(2,128)(2,1)S(1)}, bf16[1,4,1,19,2,4096]{5,4,3,2,1,0:T(2,128)(2,1)}, u32[]{:S(2)}) copy-start(bf16[1,4,1,19,2,4096]{5,4,3,2,1,0:T(2,128)(2,1)} %param.9) | copy-start | bytes 3735556
  32.5 7.0 %copy-start.1 = (bf16[2,64,2,64,1,1]{3,1,0,2,5,4:T(8,128)(2,1)S(1)}, bf16[2,64,2,64,1,1]{3,1,0,2,5,4:T(8,128)(2,1)}, u32[]{:S(2)}) copy-start(bf16[2,64,2,64,1,1]{3,1,0,2,5,4:T(8,128)(2,1)} %constant.214) | copy-start | bytes 98308
  38.9 1.2 %copy-start.2 = (f32[64,64]{0,1:T(8,128)S(1)}, f32[64,64]{0,1:T(8,128)}, u32[]{:S(2)}) copy-start(f32[64,64]{0,1:T(8,128)} %constant.121.clone) | copy-start | bytes 49156
  38.9 1.2 %copy-start.3 = (f32[64,64]{0,1:T(8,128)S(1)}, f32[64,64]{0,1:T(8,128)}, u32[]{:S(2)}) copy-start(f32[64,64]{0,1:T(8,128)} %constant.120.clone) | copy-start | bytes 49156

commit v6 on v4

--- a/solution.py
+++ b/solution.py
@@ -135,8 +135,8 @@
     return pl.pallas_call(
         functools.partial(exchange_kernel, owners, sections),
         out_shape=jax.ShapeDtypeStruct((2, sections) + blocks.shape, blocks.dtype),
-        in_specs=[pl.BlockSpec(memory_space=pltpu.VMEM)],
-        out_specs=pl.BlockSpec(memory_space=pltpu.VMEM),
+        in_specs=[pl.BlockSpec(memory_space=pl.ANY)],
+        out_specs=pl.BlockSpec(memory_space=pl.ANY),
         scratch_shapes=[
             pltpu.SemaphoreType.DMA((owners,)),
             pltpu.SemaphoreType.DMA((owners,)),
@@ -228,7 +228,7 @@
     depth = sections * owners * rows
     width = groups * AVG
     count = weights.shape[0]
-    nb = 50
+    nb = 100
     while count % nb or nb * frames * depth > 400 * 1024:
         nb -= 1
     blocks = count // nb

time: 64.9 us -> 62.4 us (0.961)
  Pallas kernels: 43.8 us -> 41.6 us
    pallas_call x1, Pallas kernels: 17.8 us -> 16.3 us  [products(): pl.pallas_call(functools.partial(product_kernel, frames, stations, mean_f...]
    pallas_call x1, Pallas kernels: 26 us -> 25.3 us  [exchange(): pl.pallas_call(functools.partial(exchange_kernel, owners, sections), out_...]
where the time goes in v6:
time: 62.4 us; the launch traced here: 62.2 us
  Pallas kernels  41.6 us (67%)
  other arithmetic  10.7 us (17%)
  local copies, waits for them, and re-layouts  8.06 us (13%)
  matrix products  0.95 us (2%)
  between operations  0.85 us (1%)
    pallas_call x1, Pallas kernels, exchange(): pl.pallas_call(functools.partial(exchange_kernel, owners, sections), out_...  25.3 us
    pallas_call x1, Pallas kernels, products(): pl.pallas_call(functools.partial(product_kernel, frames, stations, mean_f...  16.3 us
    add x1, other arithmetic, channelise(): filtered + filter_taps[tap_index] * samples[:, tap_index:tap_index + frames]  6.31 us
    slice x1, local copies, waits for them, and re-layouts, channelise(): filtered = filter_taps[0] * samples[:, 0:frames]  2.09 us
    convert_element_type x3, local copies, waits for them, and re-layouts, channelise(): (segment_two.reshape(stations, 2, frames, ROOT * ROOT) * (1.0 / ROOT)).as...  1.35 us
    select_n x1, local copies, waits for them, and re-layouts, on_device(): regrouped = jnp.take(grouped, block_owner, axis=3)  1.32 us

profile of v6, /device:TPU:0, one launch (start us, length us, event | category | flops | bytes accessed | tf_op | source)
XLA Modules:
  0.0 62.2 jit_solution(13745737800511748005)
XLA Ops:
  0.6 0.0 copy-start
  0.6 0.0 copy-start.1
  0.7 0.7 %pad_add_fusion.place_ref = s32[2]{0:T(128)} fusion(s32[1]{0:T(128)} %bitcast.1, s32[1]{0:T(128)} %bitcast), kind=kLoop, calls=%fused_computation.75 | loop fusion | flops 2 | bytes 16 | tf_op jit(solution)/shard_map/stack | solution.py:239
  1.3 0.7 %compare_and_fusion = pred[32]{0:T(512)(128)(4,1)S(1)} fusion(s32[32]{0:T(128)} %param.13), kind=kLoop, calls=%fused_computation.74 | loop fusion | flops 192 | bytes 160 | tf_op jit(solution)/shard_map/jit(_take)/and | solution.py:282
  2.0 0.7 %compare_select_fusion = s32[32]{0:T(128)S(1)} fusion(s32[32]{0:T(128)} %param.13), kind=kLoop, calls=%fused_computation.64 | loop fusion | flops 96 | bytes 256 | tf_op jit(solution)/shard_map/jit(_take)/jit(_where)/select_n | solution.py:282
  2.6 0.8 %slice_bitcast_fusion.1 = (f32[16]{0:T(128)S(1)}, f32[16]{0:T(128)S(1)}) fusion(f32[2,16]{1,0:T(2,128)} %param.11), kind=kLoop, calls=%fused_computation.77 | loop fusion | bytes 256 | tf_op jit(solution)/shard_map/squeeze | solution.py:268
  3.4 0.0 copy-done
  3.4 0.1 constant_dynamic-slice_fusion
  3.5 0.3 select_reduce_fusion
  3.9 0.1 copy.24
  4.0 0.8 %convert_element_type.24.w_ref = bf16[5,100,64]{2,1,0:T(8,128)(2,1)} reshape(bf16[250,2,64]{2,1,0:T(2,128)(2,1)S(1)} %copy.24) | data formatting | bytes 128000 | tf_op jit(solution)/shard_map/convert_element_type | solution.py:272
  4.9 0.6 %fusion.21.col_ref = bf16[64,512]{1,0:T(8,128)(2,1)} fusion(s32[512]{0:T(512)S(1)} %fusion.28), kind=kLoop, calls=%fused_computation.42 | loop fusion | flops 65536 | bytes 67584 | tf_op jit(solution)/shard_map/convert_element_type | solution.py:238
  5.5 2.1 %fusion.36 = (f32[1,4096]{1,0:T(1,128)S(1)}, f32[1,4096]{1,0:T(1,128)S(1)}, f32[1,4096]{1,0:T(1,128)S(1)}, f32[1,4096]{1,0:T(1,128)S(1)}, f32[1,4096]{1,0:T(1,12...) fusion(f32[12,4096]{1,0:T(8,128)} %param.10), kind=kLoop, calls=%fused_computation.80 | loop fusion | bytes 393216 | tf_op jit(solution)/shard_map/slice | solution.py:34
  7.6 0.0 copy-done.1
  7.6 1.1 %bitcast_convert_fusion = f32[4,19,2,4096]{3,2,1,0:T(2,128)S(1)} fusion(bf16[1,4,1,19,2,4096]{5,4,3,2,1,0:T(2,128)(2,1)S(1)} %copy-done.1), kind=kLoop, calls=%fused_computation.11 | loop fusion | flops 622592 | bytes 3735552 | tf_op jit(solution)/shard_map/convert_element_type | solution.py:31
  8.7 0.0 copy-start.2
  8.7 6.3 %fusion.10 = bf16[4,8,2,4096]{3,2,1,0:T(2,128)(2,1)S(1)} fusion(f32[4,19,2,4096]{3,2,1,0:T(2,128)S(1)} %bitcast_convert_fusion, f32[4096]{0:T(1024)S(1)} %bitcast.79, f32[4096]{0:T(1024)S(1)} %bitcast.80, f32[4096]{0:T(1024)S(1)} %bitcast.70, f32[4096]{0:T(1024)S(1)} %bitcast.71, f32[4096]{0:T(1024)S(1)} %bitcast.72, f32[4096]{0:T(1024)S(1)} %bitcast.73, ...), kind=kLoop, calls=%fused_computation.13 | loop fusion | flops 6291456 | bytes 13303808 | tf_op jit(solution)/shard_map/add | solution.py:36
  15.0 0.0 copy-start.3
  15.0 0.0 copy-start.4
  15.0 0.7 %reshape.150 = bf16[4,8,2,64,64]{4,3,2,1,0:T(8,128)(2,1)S(1)} reshape(bf16[4,8,2,4096]{3,2,1,0:T(2,128)(2,1)S(1)} %fusion.10) | data formatting | bytes 1048576 | tf_op jit(solution)/shard_map/reshape | solution.py:38
  15.7 0.0 copy-done.2
  15.7 0.5 fusion.6
  16.2 0.0 copy-done.3
  16.2 0.0 copy-done.4
  16.2 0.3 multiply_add_fusion
  16.5 0.5 fusion.9
  17.0 0.7 %copy.27 = bf16[4,2,8,64,64]{4,3,2,1,0:T(8,128)(2,1)S(1)} copy(bf16[4,2,8,64,64]{3,4,1,2,0:T(8,128)(2,1)S(1)} %fusion.9) | data formatting | bytes 1048576 | tf_op jit(solution)/shard_map/convert_element_type | solution.py:49
  17.7 0.5 convert_element_type.30
  18.1 0.2 copy.28
  18.4 0.8 %gather_fusion = bf16[32,4,2,8,128]{4,3,2,1,0:T(8,128)(2,1)S(1)} fusion(bf16[4,2,8,32,128]{4,2,3,1,0:T(8,128)(2,1)S(1)} %copy.28, s32[1024]{0:T(1024)S(1)} %pad_clamp_fusion), kind=kCustom, calls=%fused_computation | custom fusion | bytes 1048704 | tf_op jit(solution)/shard_map/jit(_take)/gather | solution.py:282
  19.2 0.1 select_bitcast_fusion
  19.3 1.3 %copy.29 = bf16[32,8,4,2,128]{4,3,2,1,0:T(2,128)(2,1)} copy(bf16[32,8,4,2,128]{4,1,3,2,0:T(8,128)(2,1)S(1)} %select_bitcast_fusion) | data formatting | bytes 1048576 | tf_op jit(solution)/shard_map/jit(_take)/select_n | solution.py:282
  20.6 25.3 %exchange.1.g_ref = bf16[2,2,4,8,64,128]{5,4,3,2,1,0:T(8,128)(2,1)} custom-call(bf16[4,8,64,128]{3,2,1,0:T(8,128)(2,1)} %bitcast.68), custom_call_target="tpu_custom_call" | custom-call | tf_op jit(solution)/shard_map/exchange/pallas_call | solution.py:135
  45.9 16.3 %products.1 = (f32[8,2,16,64]{3,2,1,0:T(8,128)}, f32[4000,1024]{1,0:T(8,128)}) custom-call(s32[2]{0:T(128)} %pad_add_fusion.place_ref, bf16[5,100,64]{2,1,0:T(8,128)(2,1)} %convert_element_type.24.w_ref, bf16[64,512]{1,0:T(8,128)(2,1)} %fusion.21.col_ref, bf16[2,2,4,8,64,128]{5,4,3,2,1,0:T(8,128)(2,1)} %exchange.1.g_ref), custom_call_target="tpu_custom_call" | custom-call | tf_op jit(solution)/shard_map/products/pallas_call | solution.py:241
  (5 shorter events, 0.1 us)
Async XLA Ops:
  0.6 2.8 %copy-start = (s32[500,32]{0,1:T(8,128)S(1)}, s32[500,32]{0,1:T(8,128)}, u32[]{:S(2)}) copy-start(s32[500,32]{0,1:T(8,128)} %param.12) | copy-start | bytes 192004
  0.6 6.9 %copy-start.1 = (bf16[1,4,1,19,2,4096]{5,4,3,2,1,0:T(2,128)(2,1)S(1)}, bf16[1,4,1,19,2,4096]{5,4,3,2,1,0:T(2,128)(2,1)}, u32[]{:S(2)}) copy-start(bf16[1,4,1,19,2,4096]{5,4,3,2,1,0:T(2,128)(2,1)} %param.9) | copy-start | bytes 3735556
  8.7 7.0 %copy-start.2 = (bf16[2,64,2,64,1,1]{3,1,0,2,5,4:T(8,128)(2,1)S(1)}, bf16[2,64,2,64,1,1]{3,1,0,2,5,4:T(8,128)(2,1)}, u32[]{:S(2)}) copy-start(bf16[2,64,2,64,1,1]{3,1,0,2,5,4:T(8,128)(2,1)} %constant.174) | copy-start | bytes 98308
  15.0 1.2 %copy-start.3 = (f32[64,64]{0,1:T(8,128)S(1)}, f32[64,64]{0,1:T(8,128)}, u32[]{:S(2)}) copy-start(f32[64,64]{0,1:T(8,128)} %constant.95.clone) | copy-start | bytes 49156
  15.0 1.2 %copy-start.4 = (f32[64,64]{0,1:T(8,128)S(1)}, f32[64,64]{0,1:T(8,128)}, u32[]{:S(2)}) copy-start(f32[64,64]{0,1:T(8,128)} %constant.94.clone) | copy-start | bytes 49156
